TPU v7x, 128 devices: a whole 4x4x4 slice. The times are simulated.
128 devices in a mesh: dp: 32 (over x, y, core), psg: 4 (over z).
Axes of the slice: x: 4, y: 4, z: 4, core: 2. Of those that a mesh axis runs over, the one named last changes fastest.
Arguments:
- query_states: bfloat16 [4096, 4096], P('dp'), may hold values from -6 to 6
- passage_last_states: bfloat16 [65536, 4096], P(('dp', 'psg')), may hold values from -6 to 6
- head_weight: bfloat16 [4096, 2048], P(None, 'psg'), may hold values from -0.09375 to 0.09375
- negatives: int32 [4, 512, 2], P(None, 'dp'), may hold values from 0 to 31, all different within a row; in each aligned block of 16 rows (0 to 15, 16 to 31, ..., all dimensions but the last counted through in order) at most 2 rows name the same one
- positives: int32 [4096], P('dp'), may hold values from 0 to 511
Outputs:
- losses: float32 [4096], P(('dp', 'psg'))
- grad_weight: bfloat16 [4096, 2048], P(None, 'psg')
Inputs may be any that keep to these rules, and one draw needn't show every extreme that they name: `negatives`: for each c and each aligned group of 16 query blocks (those of one dp index), no dp index appears more than 2 times among their column-c entries, and some reaches 2; the 2 entries of one row differ.
All inputs are finite; a program needn't handle non-finite values.
Results may differ from a plain program's by a relative error of at most 0.012.
Values may be sent and summed in bfloat16 or wider, within the bound.
No kernel may reach another device: no remote copies, remote signals or barrier semaphores. Data moves between devices by JAX's collectives and lax.ppermute only.
A program may use at most 128 MiB of HBM per device.

v0:
```python
import jax
import jax.numpy as jnp
from jax import lax
from jax.sharding import PartitionSpec as P

CAP = 2


INV_TAU = 50.0


def contract_rows(left, right):
    return lax.dot_general(
        left, right, (((0,), (0,)), ((), ())), preferred_element_type=jnp.float32
    )


def soft_terms(total, chosen):
    scaled = total * INV_TAU
    logsum = jnp.log(jnp.sum(jnp.exp(scaled), axis=(1, 2, 3)))
    groups, slots, width = (total.shape[1], total.shape[2], total.shape[3])
    corner = (
        lax.broadcasted_iota(jnp.int32, (groups, slots), 0)
        + lax.broadcasted_iota(jnp.int32, (groups, slots), 1)
        == 0
    )
    column_slot = lax.broadcasted_iota(jnp.int32, (total.shape[0], width), 1) == chosen[:, None]
    target = (corner[None, :, :, None] & column_slot[:, None, None, :]).astype(jnp.float32)
    positive = jnp.sum(scaled * target, axis=(1, 2, 3))
    grads = (jnp.exp(scaled - logsum[:, None, None, None]) - target).astype(jnp.bfloat16)
    return (logsum - positive, grads)


def shards(query_states, passage_last_states, head_weight, negatives, positives):
    groups = lax.axis_size("psg")
    ranks = lax.axis_size("dp")
    rows_query = query_states.shape[0]
    blocks_dev = negatives.shape[1]
    per_block = rows_query // blocks_dev
    width = passage_last_states.shape[0]
    slots = negatives.shape[2]
    features = head_weight.shape[1]
    share = rows_query // groups
    raw_query = jnp.dot(query_states, head_weight, preferred_element_type=jnp.float32)
    group_states = lax.all_gather(passage_last_states, "psg", axis=0, tiled=True)
    unprojected_passage = jnp.dot(group_states, head_weight, preferred_element_type=jnp.float32)
    square_query, square_passage = lax.psum(
        (
            jnp.sum(raw_query * raw_query, axis=1),
            jnp.sum(unprojected_passage * unprojected_passage, axis=1),
        ),
        "psg",
    )
    scale_query = (1.0 / jnp.sqrt(square_query + 1e-06))[:, None]
    scale_passage = (1.0 / jnp.sqrt(square_passage + 1e-06))[:, None]
    unit_query = raw_query * scale_query
    unit_passage = unprojected_passage * scale_passage
    emb_query = unit_query.astype(jnp.bfloat16)
    passage_blocks = unit_passage.astype(jnp.bfloat16).reshape(groups, width, features)
    dest_hot = (
        negatives[..., None] == lax.broadcasted_iota(jnp.int32, (1, 1, 1, ranks), 3)
    ).astype(jnp.int32)
    block_count = jnp.sum(dest_hot, axis=2)
    earlier = jnp.cumsum(block_count, axis=1) - block_count
    place = jnp.sum(earlier[:, :, None, :] * dest_hot, axis=3)
    place_hot = (place[..., None] == lax.broadcasted_iota(jnp.int32, (1, 1, 1, CAP), 3)).astype(
        jnp.int32
    )
    block_routing = (dest_hot[..., :, None] * place_hot[..., None, :]).astype(jnp.bfloat16)
    routing_exact = block_routing.astype(jnp.float32)
    query_block_list = emb_query.reshape(blocks_dev, per_block, features)
    outgoing = jnp.einsum(
        "uzfoi,zhk->ouihk", block_routing, query_block_list, preferred_element_type=jnp.float32
    ).astype(jnp.bfloat16)
    received = lax.all_to_all(outgoing, "dp", split_axis=0, concat_axis=0, tiled=True)
    partial_value = jnp.einsum(
        "scrqd,cnd->scrqn", received, passage_blocks, preferred_element_type=jnp.float32
    )
    received, partial_back = (
        received,
        lax.all_to_all(partial_value, "dp", split_axis=0, concat_axis=0, tiled=True),
    )
    local_scores = jnp.einsum(
        "cbsjr,jcrqn->bqcsn", routing_exact, partial_back, precision=lax.Precision.HIGHEST
    )
    local_scores = local_scores.reshape(rows_query, groups, slots, width)
    total = lax.psum(local_scores, "psg")
    losses, grads = soft_terms(total, positives)
    loss_out = lax.dynamic_slice_in_dim(losses, lax.axis_index("psg") * share, share, 0)
    grads = grads.reshape(blocks_dev, per_block, groups, slots, width)
    grad_out = jnp.einsum(
        "cbsjr,bqcsn->jcrqn", block_routing, grads, preferred_element_type=jnp.float32
    ).astype(jnp.bfloat16)
    arrived = lax.all_to_all(grad_out, "dp", split_axis=0, concat_axis=0, tiled=True)
    terms = (
        jnp.einsum("scrqn,cnd->scrqd", arrived, passage_blocks, preferred_element_type=jnp.float32)
        * INV_TAU
    ).astype(jnp.bfloat16)
    arrived, query_loss_terms = (
        arrived,
        lax.all_to_all(terms, "dp", split_axis=0, concat_axis=0, tiled=True),
    )
    passage_gradient = (
        jnp.einsum("scrqn,scrqd->cnd", arrived, received, preferred_element_type=jnp.float32)
        * INV_TAU
    )
    passage_gradient = passage_gradient.reshape(groups * width, features)
    d_query = jnp.einsum(
        "lkfhv,hlvaw->kaw", block_routing, query_loss_terms, preferred_element_type=jnp.float32
    ).reshape(rows_query, features)
    inner_query, inner_passage = lax.psum(
        (jnp.sum(unit_query * d_query, axis=1), jnp.sum(unit_passage * passage_gradient, axis=1)),
        "psg",
    )
    d_raw_query = ((d_query - unit_query * inner_query[:, None]) * scale_query).astype(jnp.bfloat16)
    d_raw_passage = (
        (passage_gradient - unit_passage * inner_passage[:, None]) * scale_passage
    ).astype(jnp.bfloat16)
    partial_weight = contract_rows(query_states, d_raw_query)
    partial_weight = partial_weight + contract_rows(group_states, d_raw_passage)
    grad_weight = lax.psum(partial_weight, "dp").astype(jnp.bfloat16)
    return (loss_out, grad_weight)


def solution(mesh):
    return jax.shard_map(
        shards,
        mesh=mesh,
        in_specs=(
            P("dp", None),
            P(("dp", "psg"), None),
            P(None, "psg"),
            P(None, "dp", None),
            P("dp"),
        ),
        out_specs=(P(("dp", "psg")), P(None, "psg")),
        check_vma=False,
    )
```

profile of v0, /device:TPU:1, one launch (start us, length us, event | category | flops | bytes accessed | tf_op | source)
XLA Modules:
  0.0 631.1 jit_solution(3819446292414498261)
XLA Ops:
  7.2 0.0 all-gather.2.cloned.1.call-start
  7.2 0.7 all-gather.2.cloned.1.call-update
  8.0 0.1 fusion.44
  8.1 0.3 select_reduce_fusion
  8.4 0.1 fusion.43
  8.5 0.1 convert_reduce_fusion
  8.6 3.0 multiply_reduce_fusion.1
  11.6 155.5 %all-gather.2.cloned.1.call-done = bf16[2048,4096]{1,0:T(8,128)(2,1)} async-done(((bf16[512,4096]{1,0:T(8,128)(2,1)}), bf16[2048,4096]{1,0:T(8,128)(2,1)}) %all-gather.2.cloned.1.call-update) | async-done | bytes 16777232 | tf_op jit(solution)/shard_map/all_gather | solution.py:45
  167.1 14.9 %multiply_reduce_fusion = (f32[2048]{0:T(1024)S(1)}, f32[2048,512]{1,0:T(8,128)}) fusion(bf16[2048,4096]{1,0:T(8,128)(2,1)} %all-gather.2.cloned.1.call-done, bf16[4096,512]{1,0:T(8,128)(2,1)} %param.7), kind=kOutput, calls=%fused_computation.11 | convolution fusion | flops 8592029696 | bytes 25174016 | tf_op jit(solution)/shard_map/dot_general | solution.py:46
  182.0 7.5 %all-reduce.1 = (f32[2048]{0:T(1024)S(1)}, f32[128]{0:T(128)S(1)}) all-reduce(f32[2048]{0:T(1024)S(1)} %get-tuple-element.16, f32[128]{0:T(128)S(1)} %get-tuple-element.18), channel_id=1, replica_groups=mesh['dp'=32,'psg'=4] {'psg'}, use_global_device_ids=true, to_apply=%region_1.0 | all-reduce | flops 2176 | bytes 17408 | tf_op jit(solution)/shard_map/psum | solution.py:47
  189.5 0.1 fusion.29
  189.6 0.7 convert_bitcast_fusion
  190.4 3.5 copy.20
  193.9 9.7 %all-to-all-start = ((bf16[32,4,2,8,512]{4,2,1,3,0:T(2,128)(2,1)}), bf16[32,4,2,8,512]{4,2,1,3,0:T(2,128)(2,1)S(1)}, u32[]{:S(2)}, u32[]{:S(2)}) async-start(bf16[32,4,2,8,512]{4,2,1,3,0:T(2,128)(2,1)} %copy.20), calls=%async_computation | async-start | bytes 4194304 | tf_op jit(solution)/shard_map/all_to_all | solution.py:75
  203.6 0.6 all-reduce.5.cloned.1.call-start
  204.1 3.9 multiply_convert_fusion.1
  208.0 23.8 %all-to-all-done = bf16[32,4,2,8,512]{4,2,1,3,0:T(2,128)(2,1)S(1)} async-done(((bf16[32,4,2,8,512]{4,2,1,3,0:T(2,128)(2,1)}), bf16[32,4,2,8,512]{4,2,1,3,0:T(2,128)(2,1)S(1)}, u32[]{:S(2)}, u32[]{:S(2)}) %all-to-all-start) | async-done | bytes 2097184 | tf_op jit(solution)/shard_map/all_to_all | solution.py:75
  231.9 3.2 convolution_bitcast_fusion
  235.0 3.2 copy.22
  238.3 54.5 %all_to_all.20 = f32[32,4,2,8,512]{4,2,3,1,0:T(2,128)S(1)} all-to-all(f32[32,4,2,8,512]{4,2,3,1,0:T(2,128)S(1)} %copy.22), channel_id=1, replica_groups=mesh['dp'=32,'psg'=4] {'dp'}, dimensions={0} | all-to-all | bytes 8388608 | tf_op jit(solution)/shard_map/all_to_all | solution.py:81
  292.7 4.2 fusion.17
  296.9 2.5 copy.87
  299.4 0.5 add_compare_fusion
  300.0 0.8 iota_compare_fusion
  300.7 53.2 %all-reduce.5.cloned.1.call-done = f32[128,4,2,512]{3,0,2,1:T(8,128)} async-done(((f32[128,4,2,512]{3,0,2,1:T(8,128)}), f32[128,4,2,512]{3,0,2,1:T(8,128)}) %all-reduce.5.cloned.1.call-update) | async-done | bytes 2097168 | tf_op jit(solution)/shard_map/psum | solution.py:87
  353.9 2.5 exponential_reduce_fusion
  356.4 0.5 fusion.45
  356.9 0.6 fusion.24
  357.6 0.9 fusion.20
  358.5 2.2 copy.27
  360.6 35.9 %all_to_all.21 = bf16[32,4,2,8,512]{4,2,3,1,0:T(2,128)(2,1)S(1)} all-to-all(bf16[32,4,2,8,512]{4,2,3,1,0:T(2,128)(2,1)S(1)} %copy.27), channel_id=1, replica_groups=mesh['dp'=32,'psg'=4] {'dp'}, dimensions={0} | all-to-all | bytes 4194304 | tf_op jit(solution)/shard_map/all_to_all | solution.py:94
  396.5 1.3 copy-done.5
  397.8 1.5 fusion.14
  399.3 3.5 copy.29
  402.8 4.7 all-to-all-start.3
  407.5 0.6 dynamic_slice.3
  408.1 5.6 bitcast_multiply_fusion
  413.7 2.0 copy-done.2
  415.7 1.0 fusion
  416.7 19.1 %all-to-all-done.3 = bf16[32,4,2,8,512]{4,2,1,3,0:T(2,128)(2,1)} async-done(((bf16[32,4,2,8,512]{4,2,1,3,0:T(2,128)(2,1)}), bf16[32,4,2,8,512]{4,2,1,3,0:T(2,128)(2,1)}, u32[]{:S(2)}, u32[]{:S(2)}) %all-to-all-start.3) | async-done | bytes 2097184 | tf_op jit(solution)/shard_map/all_to_all | solution.py:101
  435.9 2.8 fusion.21
  438.7 0.2 fusion.26
  439.0 7.0 %all-reduce = (f32[128]{0:T(128)S(1)}, f32[2048]{0:T(1024)S(1)}) all-reduce(f32[128]{0:T(128)S(1)} %fusion.26, f32[2048]{0:T(1024)S(1)} %fusion), channel_id=1, replica_groups=mesh['dp'=32,'psg'=4] {'psg'}, use_global_device_ids=true, to_apply=%region_12.13 | all-reduce | flops 2176 | bytes 17408 | tf_op jit(solution)/shard_map/psum | solution.py:111
  446.0 3.9 fusion.2
  449.9 1.4 fusion.30
  451.3 15.1 %add_bitcast_fusion = f32[4096,512]{0,1:T(8,128)} fusion(f32[512,4096]{1,0:T(8,128)S(1)} %fusion.30, bf16[2048,512]{1,0:T(8,128)(2,1)S(1)} %fusion.2, bf16[2048,4096]{1,0:T(8,128)(2,1)} %all-gather.2.cloned.1.call-done), kind=kOutput, calls=%fused_computation | convolution fusion | flops 8592031744 | bytes 35651584 | tf_op jit(solution)/shard_map/dot_general | solution.py:13
  466.4 151.2 %all-reduce.6 = bf16[4096,512]{0,1:T(8,128)(2,1)} all-reduce(f32[4096,512]{0,1:T(8,128)} %add_bitcast_fusion), channel_id=1, replica_groups=mesh['dp'=32,'psg'=4] {'dp'}, use_global_device_ids=true, to_apply=%region_15.16 | all-reduce | flops 2097152 | bytes 12582912 | tf_op jit(solution)/shard_map/psum | solution.py:121
  617.6 6.4 %copy.34 = bf16[4096,512]{1,0:T(8,128)(2,1)} copy(bf16[4096,512]{0,1:T(8,128)(2,1)} %all-reduce.6) | data formatting | bytes 8388608
  (30 shorter events, 0.2 us)
Async XLA Ops:
  7.2 1.5 copy-start
  7.2 0.8 copy-start.8
  7.2 159.9 %all-gather.2.cloned.1.call-start = ((), (), s32[]{:S(2)}) async-start(), calls=%async_computation.4 | async-start | bytes 20971520 | tf_op jit(solution)/shard_map/all_gather | solution.py:45
  8.6 181.0 %copy-start.6 = (bf16[4,16,32,2]{2,1,3,0:T(8,128)(2,1)}, bf16[4,16,32,2]{2,1,3,0:T(8,128)(2,1)S(1)}, u32[]{:S(2)}) copy-start(bf16[4,16,32,2]{2,1,3,0:T(8,128)(2,1)S(1)} %convert_reduce_fusion) | copy-start | bytes 24580
  189.5 4.3 copy-start.9
  193.9 38.0 %all-to-all-start = ((bf16[32,4,2,8,512]{4,2,1,3,0:T(2,128)(2,1)}), bf16[32,4,2,8,512]{4,2,1,3,0:T(2,128)(2,1)S(1)}, u32[]{:S(2)}, u32[]{:S(2)}) async-start(bf16[32,4,2,8,512]{4,2,1,3,0:T(2,128)(2,1)} %copy.20), calls=%async_computation | async-start | bytes 4194304 | tf_op jit(solution)/shard_map/all_to_all | solution.py:75
  203.6 150.4 %all-reduce.5.cloned.1.call-start = ((), (), s32[]{:S(2)}) async-start(), calls=%async_computation.5 | async-start | bytes 4194304 | tf_op jit(solution)/shard_map/psum | solution.py:87
  353.9 3.0 copy-start.4
  353.9 3.0 copy-start.11
  360.6 37.2 %copy-start.3 = (bf16[2048,512]{1,0:T(8,128)(2,1)S(1)}, bf16[2048,512]{1,0:T(8,128)(2,1)}, u32[]{:S(2)}) copy-start(bf16[2048,512]{1,0:T(8,128)(2,1)} %multiply_convert_fusion.1) | copy-start | bytes 6291460
  396.5 1.3 copy-start.5
  402.8 4.7 copy-start.12
  402.8 33.1 %all-to-all-start.3 = ((bf16[32,4,2,8,512]{4,2,1,3,0:T(2,128)(2,1)}), bf16[32,4,2,8,512]{4,2,1,3,0:T(2,128)(2,1)}, u32[]{:S(2)}, u32[]{:S(2)}) async-start(bf16[32,4,2,8,512]{4,2,1,3,0:T(2,128)(2,1)} %copy.29), calls=%async_computation.3 | async-start | bytes 4194304 | tf_op jit(solution)/shard_map/all_to_all | solution.py:101
  408.1 7.6 %copy-start.1 = (f32[2048,512]{1,0:T(8,128)S(1)}, f32[2048,512]{1,0:T(8,128)}, u32[]{:S(2)}) copy-start(f32[2048,512]{1,0:T(8,128)} %get-tuple-element.17) | copy-start | bytes 12582916
  413.7 2.0 copy-start.2
  415.7 20.2 %copy-start.7 = (bf16[4,16,32,2]{2,1,3,0:T(8,128)(2,1)S(1)}, bf16[4,16,32,2]{2,1,3,0:T(8,128)(2,1)}, u32[]{:S(2)}) copy-start(bf16[4,16,32,2]{2,1,3,0:T(8,128)(2,1)} %copy-done.6) | copy-start | bytes 24580
  416.7 22.0 %copy-start.10 = (f32[128]{0:T(128)S(1)}, f32[128]{0:T(128)}, u32[]{:S(2)}) copy-start(f32[128]{0:T(128)} %copy-done.9) | copy-start | bytes 1540
Sparse Core Ops, SparseCore 0:
  9.7 157.3 all-gather.1
  299.6 54.3 all-reduce.4
where the time goes:
time: 641 us; the launch traced here: 631 us
  blocking collectives  256 us (40%)
  waiting for transfers between devices  252 us (39%)
  matrix products  53.2 us (8%)
  local copies, waits for them, and re-layouts  25.3 us (4%)
  starting transfers between devices  15 us (2%)
  other arithmetic  14.6 us (2%)
  between operations  14.6 us (2%)
    all_gather x1, waiting for transfers between devices, shards(): lax.all_gather(passage_last_states, 'psg', axis=0, tiled=True)  155 us
    psum x1, blocking collectives, shards(): grad_weight = lax.psum(partial_weight, 'dp').astype(jnp.bfloat16)  151 us
    all_to_all x1, blocking collectives, shards(): lax.all_to_all(partial_value, 'dp', split_axis=0, concat_axis=0, tiled=True)  54.5 us
    psum x1, waiting for transfers between devices, shards(): total = lax.psum(local_scores, 'psg')  53.2 us
    all_to_all x1, blocking collectives, shards(): lax.all_to_all(grad_out, 'dp', split_axis=0, concat_axis=0, tiled=True)  35.9 us
    all_to_all x1, waiting for transfers between devices, shards(): lax.all_to_all(outgoing, 'dp', split_axis=0, concat_axis=0, tiled=True)  23.8 us
    all_to_all x1, waiting for transfers between devices, shards(): lax.all_to_all(terms, 'dp', split_axis=0, concat_axis=0, tiled=True)  19.1 us
    dot_general x2, matrix products, contract_rows(): lax.dot_general(left, right, (((0,), (0,)), ((), ())), preferred_element_...  16.5 us
  transfers between devices with their start and end apart: 4, of which 4 were waited for; matrix products, arithmetic and copies ran while one was open for 3% of the time, Pallas kernels for 0%

commit v1 on v0

v1 whole, which is shorter than its diff:
```python
import jax
import jax.numpy as jnp
from jax import lax
from jax.sharding import PartitionSpec as P

CAP = 2
INV_TAU = 50.0
F32 = jnp.float32
BF16 = jnp.bfloat16
SIDE = 4


def dp_perm(move):
    pairs = []
    for x in range(SIDE):
        for y in range(SIDE):
            for core in range(2):
                tx, ty, tcore = move(x, y, core)
                target = ((tx % SIDE) * SIDE + ty % SIDE) * 2 + tcore
                pairs.append(((x * SIDE + y) * 2 + core, target))
    return pairs


def first(value, step):
    return lax.ppermute(
        value, "dp", dp_perm(lambda x, y, k: (x + step, y, k) if k == 0 else (x, y + step, k))
    )


def second(value, step):
    return lax.ppermute(
        value, "dp", dp_perm(lambda x, y, k: (x, y + step, k) if k == 0 else (x + step, y, k))
    )


def third(value, step):
    return lax.ppermute(value, "psg", [(c, (c + step) % SIDE) for c in range(SIDE)])


def swap(value):
    return lax.ppermute(value, "dp", dp_perm(lambda x, y, k: (x, y, 1 - k)))


def ring_scatter(chunk, move):
    far = chunk(2)
    half = far.shape[0] // 2
    from_left = move(far[:half], 1)
    from_right = move(far[half:], -1)
    right = chunk(1)
    left = chunk(3)
    right = jnp.concatenate(
        [(right[:half].astype(F32) + from_left.astype(F32)).astype(BF16), right[half:]], axis=0
    )
    left = jnp.concatenate(
        [left[:half], (left[half:].astype(F32) + from_right.astype(F32)).astype(BF16)], axis=0
    )
    from_left = move(right, 1)
    from_right = move(left, -1)
    own = chunk(0)
    return own.astype(F32) + from_left.astype(F32) + from_right.astype(F32)


def ring_gather(piece, move, place):
    half = piece.shape[0] // 2
    left = move(piece, 1)
    right = move(piece, -1)
    far = jnp.concatenate([move(left[:half], 1), move(right[half:], -1)], axis=0)
    rows = piece.shape[0]
    out = jnp.concatenate([piece, right, far, left] * 2, axis=0)
    start = lax.rem(SIDE - place, SIDE) * rows
    return lax.dynamic_slice_in_dim(out, start, SIDE * rows, 0)


def ring_sum(value, move):
    return value + move(value, 1) + move(value, -1) + move(value, 2)


def project(states, pieces):
    return [jnp.dot(states, piece, preferred_element_type=F32) for piece in pieces]


def routes(mine, per_block, ranks):
    blocks, slots = mine.shape
    same = (mine[:, :, None, None] == mine[None, None, :, :]).astype(jnp.int32)
    before = (
        lax.broadcasted_iota(jnp.int32, (blocks, blocks), 1)
        < lax.broadcasted_iota(jnp.int32, (blocks, blocks), 0)
    ).astype(jnp.int32)
    place = jnp.sum(same * before[:, None, :, None], axis=(2, 3))
    line = mine * CAP + place
    rows = ranks * CAP * per_block
    line = jnp.repeat(line, per_block, axis=0)
    count = blocks * per_block
    row = lax.broadcasted_iota(jnp.int32, (rows, count), 0)
    col = lax.broadcasted_iota(jnp.int32, (rows, count), 1)
    aligned = lax.rem(row, per_block) == lax.rem(col, per_block)
    row_line = row // per_block
    hot = [aligned & (row_line == line[None, :, s]) for s in range(slots)]
    return (hot[0] | hot[1]).astype(BF16), hot[0].astype(BF16)


def shards(query_states, passage_last_states, head_weight, negatives, positives):
    ranks = lax.axis_size("dp")
    groups = lax.axis_size("psg")
    dp = lax.axis_index("dp")
    column = lax.axis_index("psg")
    core = lax.rem(dp, 2)
    x = dp // (2 * SIDE)
    y = lax.rem(dp // 2, SIDE)
    u = jnp.where(core == 0, x, y)
    v = jnp.where(core == 0, y, x)
    queries, depth = query_states.shape
    blocks = negatives.shape[1]
    per_block = queries // blocks
    width = passage_last_states.shape[0]
    share = head_weight.shape[1]
    half = share // 2

    mine0 = lax.dynamic_slice_in_dim(head_weight, core * half, half, 1)
    theirs0 = lax.dynamic_slice_in_dim(head_weight, (1 - core) * half, half, 1)
    mine3 = third(mine0, 1)
    mine1 = third(mine0, -1)
    mine2 = jnp.concatenate(
        [third(mine3[: depth // 2], 1), third(mine1[depth // 2 :], -1)], axis=0
    )

    picked = lax.dynamic_index_in_dim(negatives, column, 0, keepdims=False)
    route, route0 = routes(picked, per_block, ranks)
    number = lax.broadcasted_iota(jnp.int32, (queries, 1), 0) // per_block
    facts = jnp.concatenate(
        [jnp.ones_like(number), number, positives[:, None] // 16, positives[:, None] % 16], axis=1
    ).astype(BF16)
    lead = jnp.where(column == 0, 1.0, 0.0).astype(BF16)
    facts = jnp.concatenate(
        [
            jnp.dot(route, facts, preferred_element_type=F32),
            jnp.sum(route0.astype(F32), axis=1, keepdims=True) * lead.astype(F32),
        ],
        axis=1,
    ).astype(BF16)
    facts = jnp.pad(facts, ((0, 0), (0, 128 - facts.shape[1])))
    outgoing = jnp.dot(route, query_states, preferred_element_type=F32).astype(BF16)
    outgoing = jnp.concatenate([outgoing, facts], axis=1)
    rows = outgoing.shape[0]
    received = lax.all_to_all(
        outgoing.reshape(ranks, rows // ranks, depth + 128),
        "dp",
        split_axis=0,
        concat_axis=0,
        tiled=True,
    ).reshape(rows, depth + 128)
    asked = received[:, :depth]
    facts = received[:, depth : depth + 8].astype(jnp.int32)
    valid = facts[:, 0] == 1
    block_of = facts[:, 1]
    chosen = jnp.where(facts[:, 4] == 1, facts[:, 2] * 16 + facts[:, 3], -1)

    other_states = swap(passage_last_states)
    other_asked = swap(asked)

    pieces = [mine0, mine1, mine2, mine3, theirs0, swap(mine1), swap(mine2), swap(mine3)]
    raw_p = jnp.concatenate(project(passage_last_states, pieces), axis=1)
    raw_q = jnp.concatenate(project(asked, pieces), axis=1)
    scale_p = 1.0 / jnp.sqrt(jnp.sum(raw_p * raw_p, axis=1, keepdims=True) + 1e-06)
    scale_q = 1.0 / jnp.sqrt(jnp.sum(raw_q * raw_q, axis=1, keepdims=True) + 1e-06)
    unit_p = raw_p * scale_p
    unit_q = raw_q * scale_q
    emb_p = unit_p.astype(BF16)
    emb_q = unit_q.astype(BF16)

    scores = (
        lax.dot_general(emb_q, emb_p, (((1,), (1,)), ((), ())), preferred_element_type=F32)
        * INV_TAU
    )
    target = (lax.broadcasted_iota(jnp.int32, (rows, width), 1) == chosen[:, None]).astype(F32)
    exps = jnp.exp(scores)
    sums = jnp.where(valid, jnp.sum(exps, axis=1), 0.0)
    hits = jnp.sum(scores * target, axis=1)

    spread = (
        block_of.reshape(ranks, CAP, 1, per_block)
        == lax.broadcasted_iota(jnp.int32, (1, 1, blocks, 1), 2)
    ).astype(F32)
    both = jnp.stack([sums, hits]).reshape(2, ranks, CAP, 1, per_block)
    both = jnp.sum(both * spread[None], axis=2)
    packed = both.reshape(-1, 128)
    packed = ring_sum(packed, first)
    packed = ring_sum(packed, second)
    packed = packed + swap(packed)
    packed = ring_sum(packed, third)
    both = packed.reshape(2, ranks, blocks, per_block)
    losses = (jnp.log(both[0]) - both[1]).reshape(-1)
    out_share = queries // groups
    loss_out = lax.dynamic_slice_in_dim(losses, (dp * groups + column) * out_share, out_share, 0)
    denom = jnp.sum(both[0][:, None] * spread, axis=2).reshape(rows)
    denom = jnp.where(valid, denom, 1.0)
    grads = (exps * (1.0 / denom)[:, None] - target).astype(BF16)

    d_q = jnp.dot(grads, emb_p, preferred_element_type=F32) * INV_TAU
    d_p = (
        lax.dot_general(grads, emb_q, (((0,), (0,)), ((), ())), preferred_element_type=F32)
        * INV_TAU
    )
    inner_q = jnp.sum(unit_q * d_q, axis=1, keepdims=True)
    inner_p = jnp.sum(unit_p * d_p, axis=1, keepdims=True)
    d_raw_q = ((d_q - unit_q * inner_q) * scale_q).astype(BF16)
    d_raw_p = ((d_p - unit_p * inner_p) * scale_p).astype(BF16)

    keep = SIDE * half
    d_mine = jnp.concatenate([d_raw_p[:, :keep], d_raw_q[:, :keep]], axis=0)
    d_other = swap(jnp.concatenate([d_raw_p[:, keep:], d_raw_q[:, keep:]], axis=0))
    d_all = jnp.concatenate([d_mine, d_other], axis=0)
    states = jnp.concatenate([passage_last_states, asked, other_states, other_asked], axis=0)
    part = depth // SIDE

    def term(step):
        place = lax.rem(u + step, SIDE)
        left = lax.dynamic_slice_in_dim(states, place * part, part, 1)
        return lax.dot_general(
            left, d_all, (((0,), (0,)), ((), ())), preferred_element_type=F32
        ).astype(BF16)

    summed = ring_scatter(term, first).astype(BF16)
    part2 = part // SIDE
    summed = ring_scatter(
        lambda step: lax.dynamic_slice_in_dim(summed, lax.rem(v + step, SIDE) * part2, part2, 0),
        second,
    ).astype(BF16)
    piece = ring_scatter(lambda step: summed[:, step * half : (step + 1) * half], third).astype(
        BF16
    )
    piece = ring_gather(piece, second, v)
    piece = ring_gather(piece, first, u)
    other = swap(piece)
    grad_weight = jnp.where(
        core == 0,
        jnp.concatenate([piece, other], axis=1),
        jnp.concatenate([other, piece], axis=1),
    )
    return (loss_out, grad_weight)


def solution(mesh):
    return jax.shard_map(
        shards,
        mesh=mesh,
        in_specs=(
            P("dp", None),
            P(("dp", "psg"), None),
            P(None, "psg"),
            P(None, "dp", None),
            P("dp"),
        ),
        out_specs=(P(("dp", "psg")), P(None, "psg")),
        check_vma=False,
    )
```

time: 641 us -> 373 us (0.58)
  blocking collectives: 256 us -> 0 us
  waiting for transfers between devices: 252 us -> 111 us
  starting transfers between devices: 15 us -> 74.5 us
  matrix products: 53.2 us -> 111 us
  other arithmetic: 14.6 us -> 39.2 us
  between operations: 14.6 us -> 1.9 us
    psum x3 -> x0, blocking collectives: 166 us -> none  [the longest x1 151 us: shards(): grad_weight = lax.psum(partial_weight, 'dp').astype(jnp.bfloat16)]
    all_gather x1 -> x0, waiting for transfers between devices: 155 us -> none  [shards(): lax.all_gather(passage_last_states, 'psg', axis=0, tiled=True)]
    ppermute x0 -> x41, waiting for transfers between devices: none -> 111 us  [the longest x11 47 us: third(): lax.ppermute(value, 'psg', [(c, (c + step) % SIDE) for c in range(SIDE)])]
    all_to_all x2 -> x0, blocking collectives: 90.3 us -> none  [the longest x1 54.5 us: shards(): lax.all_to_all(partial_value, 'dp', split_axis=0, concat_axis=0, tiled=True)]
    ppermute x0 -> x41, starting transfers between devices: none -> 66.4 us  [the longest x8 22 us: swap(): return lax.ppermute(value, 'dp', dp_perm(lambda x, y, k: (x, y, 1 - k)))]
    dot_general x11 -> x25, matrix products: 53.2 us -> 111 us  [the longest x16 66.6 us: project(): jnp.dot(states, piece, preferred_element_type=F32)]
    psum x1 -> x0, waiting for transfers between devices: 53.2 us -> none  [shards(): total = lax.psum(local_scores, 'psg')]
    all_to_all x2 -> x1, waiting for transfers between devices: 43 us -> 0.01 us  [shards(): lax.all_to_all(outgoing.reshape(ranks, rows // ranks, depth + 128), 'dp',...]
  transfers between devices with their start and end apart: 4 -> 42, of which waited for: 4 -> 24; matrix products, arithmetic and copies ran while one was open for 3% -> 35% of each run, Pallas kernels for 0% -> 0%
where the time goes in v1:
time: 373 us; the launch traced here: 367 us
  matrix products  111 us (30%)
  waiting for transfers between devices  111 us (30%)
  starting transfers between devices  74.5 us (20%)
  other arithmetic  39.2 us (11%)
  local copies, waits for them, and re-layouts  29.8 us (8%)
    dot_general x16, matrix products, project(): jnp.dot(states, piece, preferred_element_type=F32)  66.6 us
    ppermute x11, waiting for transfers between devices, third(): lax.ppermute(value, 'psg', [(c, (c + step) % SIDE) for c in range(SIDE)])  47 us
    ppermute x11, waiting for transfers between devices, first(): lax.ppermute(value, 'dp', dp_perm(lambda x, y, k: (x + step, y, k) if k =...  38.2 us
    dot_general x4, matrix products, term(): lax.dot_general(left, d_all, (((0,), (0,)), ((), ())), preferred_element_...  28 us
    ppermute x8, starting transfers between devices, swap(): return lax.ppermute(value, 'dp', dp_perm(lambda x, y, k: (x, y, 1 - k)))  22 us
    ppermute x11, waiting for transfers between devices, second(): lax.ppermute(value, 'dp', dp_perm(lambda x, y, k: (x, y + step, k) if k =...  21.1 us
    ppermute x11, starting transfers between devices, third(): lax.ppermute(value, 'psg', [(c, (c + step) % SIDE) for c in range(SIDE)])  15.9 us
    ppermute x11, starting transfers between devices, second(): lax.ppermute(value, 'dp', dp_perm(lambda x, y, k: (x, y + step, k) if k =...  15 us
  transfers between devices with their start and end apart: 42, of which 24 were waited for; matrix products, arithmetic and copies ran while one was open for 35% of the time, Pallas kernels for 0%

profile of v1, /device:TPU:1, one launch (start us, length us, event | category | flops | bytes accessed | tf_op | source)
XLA Modules:
  0.0 366.6 jit_solution(1270971983870463238)
XLA Ops:
  8.2 3.0 convolution_convert_fusion
  11.9 3.8 %fusion.1 = bf16[512,4224]{1,0:T(8,128)(2,1)} fusion(bf16[512,5]{1,0:T(8,128)(2,1)S(1)} %copy.52, bf16[512,4096]{1,0:T(8,128)(2,1)} %convolution_convert_fusion), kind=kLoop, calls=%fused_computation.4 | loop fusion | flops 12976128 | bytes 8524800 | tf_op jit(solution)/shard_map/concatenate | solution.py:143
  15.7 8.1 %all-to-all-start = ((bf16[32,16,4224]{2,1,0:T(8,128)(2,1)}), bf16[32,16,4224]{2,1,0:T(8,128)(2,1)}, u32[]{:S(2)}, u32[]{:S(2)}) async-start(bf16[32,16,4224]{2,1,0:T(8,128)(2,1)} %bitcast.79), calls=%async_computation | async-start | bytes 8650752 | tf_op jit(solution)/shard_map/all_to_all | solution.py:145
  23.8 28.8 %collective-permute-done.1 = bf16[4096,256]{1,0:T(8,128)(2,1)} collective-permute-done((bf16[4096,256]{1,0:T(8,128)(2,1)S(1)}, bf16[4096,256]{1,0:T(8,128)(2,1)}, u32[]{:S(2)}, u32[]{:S(2)}) %collective-permute-start.1) | collective-permute-done | bytes 2097184 | tf_op jit(solution)/shard_map/ppermute | solution.py:37
  56.2 2.7 collective-permute-start.3
  59.0 4.3 %fusion.38 = f32[512,2048]{0,1:T(8,128)} fusion(bf16[4096,256]{1,0:T(8,128)(2,1)S(1)} %constant_dynamic-slice_fusion.6, bf16[512,4096]{1,0:T(8,128)(2,1)} %param.6), kind=kOutput, calls=%fused_computation.60 | convolution fusion | flops 1073741824 | bytes 6815744 | tf_op jit(solution)/shard_map/dot_general | solution.py:79
  65.0 3.7 %fusion.37 = f32[512,2048]{0,1:T(8,128)} fusion(f32[512,2048]{0,1:T(8,128)} %fusion.38, bf16[4096,256]{1,0:T(8,128)(2,1)} %collective-permute-done, bf16[512,4096]{1,0:T(8,128)(2,1)S(1)} %copy-done.6), kind=kOutput, calls=%fused_computation.58 | convolution fusion | flops 1073741824 | bytes 6815744 | tf_op jit(solution)/shard_map/dot_general | solution.py:79
  68.7 11.0 %collective-permute-done.2 = bf16[2048,256]{1,0:T(8,128)(2,1)S(1)} collective-permute-done((bf16[2048,256]{1,0:T(8,128)(2,1)}, bf16[2048,256]{1,0:T(8,128)(2,1)S(1)}, u32[]{:S(2)}, u32[]{:S(2)}) %collective-permute-start.2) | collective-permute-done | bytes 1048608 | tf_op jit(solution)/shard_map/ppermute | solution.py:37
  84.2 3.7 %fusion.36 = f32[512,2048]{0,1:T(8,128)} fusion(f32[512,2048]{0,1:T(8,128)} %fusion.37, bf16[4096,256]{1,0:T(8,128)(2,1)} %constant_dynamic-update-slice_fusion, bf16[512,4096]{1,0:T(8,128)(2,1)S(1)} %copy-done.6), kind=kOutput, calls=%fused_computation.56 | convolution fusion | flops 1073741824 | bytes 6815744 | tf_op jit(solution)/shard_map/dot_general | solution.py:79
  87.9 3.8 %fusion.35 = f32[512,2048]{0,1:T(8,128)} fusion(f32[512,2048]{0,1:T(8,128)} %fusion.36, bf16[4096,256]{1,0:T(8,128)(2,1)} %collective-permute-done.1, bf16[512,4096]{1,0:T(8,128)(2,1)S(1)} %copy-done.6), kind=kOutput, calls=%fused_computation.54 | convolution fusion | flops 1073741824 | bytes 6815744 | tf_op jit(solution)/shard_map/dot_general | solution.py:79
  95.4 4.3 %convolution_dynamic-update-slice_fusion.6 = f32[512,2048]{0,1:T(8,128)} fusion(bf16[4096,256]{1,0:T(8,128)(2,1)S(1)} %constant_dynamic-slice_fusion.6, bf16[512,4224]{1,0:T(8,128)(2,1)} %bitcast.6), kind=kOutput, calls=%fused_computation.44 | convolution fusion | flops 1073741824 | bytes 6815744 | tf_op jit(solution)/shard_map/dot_general | solution.py:79
  100.0 5.0 %convolution_dynamic-update-slice_fusion.5 = f32[512,2048]{0,1:T(8,128)} fusion(f32[512,2048]{0,1:T(8,128)} %convolution_dynamic-update-slice_fusion.6, bf16[4096,256]{1,0:T(8,128)(2,1)} %collective-permute-done, bf16[512,4224]{1,0:T(8,128)(2,1)} %bitcast.6), kind=kOutput, calls=%fused_computation.43 | convolution fusion | flops 1073741824 | bytes 6815744 | tf_op jit(solution)/shard_map/dot_general | solution.py:79
  105.0 5.0 %convolution_dynamic-update-slice_fusion.4 = f32[512,2048]{0,1:T(8,128)} fusion(f32[512,2048]{0,1:T(8,128)} %convolution_dynamic-update-slice_fusion.5, bf16[4096,256]{1,0:T(8,128)(2,1)} %constant_dynamic-update-slice_fusion, bf16[512,4224]{1,0:T(8,128)(2,1)} %bitcast.6), kind=kOutput, calls=%fused_computation.42 | convolution fusion | flops 1073741824 | bytes 6815744 | tf_op jit(solution)/shard_map/dot_general | solution.py:79
  110.0 5.1 %convolution_dynamic-update-slice_fusion.3 = f32[512,2048]{0,1:T(8,128)} fusion(f32[512,2048]{0,1:T(8,128)} %convolution_dynamic-update-slice_fusion.4, bf16[4096,256]{1,0:T(8,128)(2,1)} %collective-permute-done.1, bf16[512,4224]{1,0:T(8,128)(2,1)} %bitcast.6), kind=kOutput, calls=%fused_computation.41 | convolution fusion | flops 1073741824 | bytes 6815744 | tf_op jit(solution)/shard_map/dot_general | solution.py:79
  115.1 4.5 %fusion.23 = f32[512,2048]{0,1:T(8,128)} fusion(f32[512,2048]{0,1:T(8,128)} %convolution_dynamic-update-slice_fusion.3, bf16[4096,512]{1,0:T(8,128)(2,1)S(1)} %copy-done.9, s32[]{:T(128)S(6)} %select_n.134, bf16[512,4224]{1,0:T(8,128)(2,1)} %bitcast.6), kind=kOutput, calls=%fused_computation.37 | convolution fusion | flops 1073741824 | bytes 6815748 | tf_op jit(solution)/shard_map/dot_general | solution.py:79
  119.6 3.9 %fusion.34 = f32[512,2048]{0,1:T(8,128)} fusion(f32[512,2048]{0,1:T(8,128)} %fusion.29, bf16[4096,256]{1,0:T(8,128)(2,1)} %collective-permute-done.4, bf16[512,4096]{1,0:T(8,128)(2,1)S(1)} %copy-done.7), kind=kOutput, calls=%fused_computation.52 | convolution fusion | flops 1073741824 | bytes 6815744 | tf_op jit(solution)/shard_map/dot_general | solution.py:79
  123.5 4.4 %convolution_dynamic-update-slice_fusion.2 = f32[512,2048]{0,1:T(8,128)S(1)} fusion(f32[512,2048]{0,1:T(8,128)S(1)} %copy-done.2, bf16[4096,256]{1,0:T(8,128)(2,1)} %collective-permute-done.4, bf16[512,4224]{1,0:T(8,128)(2,1)} %bitcast.6), kind=kOutput, calls=%fused_computation.40 | convolution fusion | flops 1073741824 | bytes 6815744 | tf_op jit(solution)/shard_map/dot_general | solution.py:79
  127.9 4.2 %convolution_dynamic-update-slice_fusion.1 = f32[512,2048]{0,1:T(8,128)S(1)} fusion(f32[512,2048]{0,1:T(8,128)S(1)} %convolution_dynamic-update-slice_fusion.2, bf16[4096,256]{1,0:T(8,128)(2,1)} %collective-permute-done.5, bf16[512,4224]{1,0:T(8,128)(2,1)} %bitcast.6), kind=kOutput, calls=%fused_computation.39 | convolution fusion | flops 1073741824 | bytes 6815744 | tf_op jit(solution)/shard_map/dot_general | solution.py:79
  132.1 4.2 %convolution_dynamic-update-slice_fusion = f32[512,2048]{0,1:T(8,128)S(1)} fusion(f32[512,2048]{0,1:T(8,128)S(1)} %convolution_dynamic-update-slice_fusion.1, bf16[4096,256]{1,0:T(8,128)(2,1)} %collective-permute-done.6, bf16[512,4224]{1,0:T(8,128)(2,1)} %bitcast.6), kind=kOutput, calls=%fused_computation.38 | convolution fusion | flops 1073741824 | bytes 6815744 | tf_op jit(solution)/shard_map/dot_general | solution.py:79
  136.6 4.9 %fusion.33 = f32[512,2048]{0,1:T(8,128)} fusion(f32[512,2048]{0,1:T(8,128)} %fusion.34, bf16[4096,256]{1,0:T(8,128)(2,1)} %collective-permute-done.5, bf16[512,4096]{1,0:T(8,128)(2,1)S(1)} %copy-done.7), kind=kOutput, calls=%fused_computation.50 | convolution fusion | flops 1073741824 | bytes 6815744 | tf_op jit(solution)/shard_map/dot_general | solution.py:79
  141.5 3.7 %fusion.32 = f32[512,2048]{0,1:T(8,128)} fusion(f32[512,2048]{0,1:T(8,128)} %fusion.33, bf16[4096,256]{1,0:T(8,128)(2,1)} %collective-permute-done.6, bf16[512,4096]{1,0:T(8,128)(2,1)S(1)} %copy-done.7), kind=kOutput, calls=%fused_computation.48 | convolution fusion | flops 1073741824 | bytes 6815744 | tf_op jit(solution)/shard_map/dot_general | solution.py:79
  147.7 3.7 %exponential_reduce_fusion = (f32[512]{0:T(512)S(1)}, f32[512]{0:T(512)S(1)}, f32[512,512]{0,1:T(8,128)S(1)}) fusion(s32[512]{0:T(512)S(1)} %get-tuple-element.4, f32[512,2048]{0,1:T(8,128)} %fusion.32, f32[512]{0:T(512)S(1)} %add_rsqrt_fusion, f32[512,2048]{0,1:T(8,128)S(1)} %convolution_dynamic-update-slice_fusion, f32[512]{0:T(512)S(1)} %add_rsqrt_fusion.1), kind=kOutput, calls=%fused_computation.66 | convolution fusion | flops 1079245824 | bytes 9447424 | tf_op jit(solution)/shard_map/dot_general | solution.py:172
  152.2 3.0 collective-permute-start.9
  159.9 2.8 collective-permute-start.12
  167.6 3.5 collective-permute-start.13
  176.6 4.7 %slice.174 = bf16[512,4096]{1,0:T(8,128)(2,1)} slice(bf16[512,4224]{1,0:T(8,128)(2,1)} %bitcast.6), slice={[0:512], [0:4096]} | slice | bytes 8388608 | tf_op jit(solution)/shard_map/slice | solution.py:152
  182.0 5.1 %multiply_reduce_fusion.1 = (f32[512]{0:T(512)S(1)}, f32[512,2048]{0,1:T(8,128)S(1)}) fusion(f32[512,2048]{0,1:T(8,128)} %fusion.32, f32[512]{0:T(512)S(1)} %add_rsqrt_fusion, f32[512,2048]{0,1:T(8,128)} %copy-done.3, f32[512]{0:T(512)S(1)} %add_rsqrt_fusion.1, f32[512,512]{0,1:T(8,128)S(1)} %get-tuple-element.36, f32[512]{0:T(512)S(1)} %fusion.43, ...), kind=kOutput, calls=%fused_computation.17 | convolution fusion | flops 1081343488 | bytes 13641728 | tf_op jit(solution)/shard_map/dot_general | solution.py:201
  187.0 3.4 multiply_convert_fusion.1
  193.0 3.8 %multiply_reduce_fusion = (f32[512]{0:T(512)S(1)}, f32[512,2048]{0,1:T(8,128)S(1)}) fusion(f32[512,2048]{0,1:T(8,128)S(1)} %copy-done.4, f32[512]{0:T(512)S(1)} %add_rsqrt_fusion.1, f32[512,512]{0,1:T(8,128)S(1)} %get-tuple-element.36, f32[512]{0:T(512)S(1)} %fusion.43, s32[512]{0:T(512)S(1)} %get-tuple-element.4, f32[512,2048]{0,1:T(8,128)} %fusion.32, ...), kind=kOutput, calls=%fused_computation.15 | convolution fusion | flops 1081343488 | bytes 13641728 | tf_op jit(solution)/shard_map/dot_general | solution.py:199
  200.2 8.7 %pad_maximum_fusion = bf16[2048,4096]{1,0:T(8,128)(2,1)S(1)} fusion(bf16[512,4096]{1,0:T(8,128)(2,1)} %collective-permute-done.18, bf16[512,4096]{1,0:T(8,128)(2,1)} %collective-permute-done.17, bf16[512,4096]{1,0:T(8,128)(2,1)} %slice.174, bf16[512,4096]{1,0:T(8,128)(2,1)} %param.6), kind=kLoop, calls=%fused_computation | loop fusion | flops 67108864 | bytes 33554432 | tf_op jit(solution)/shard_map/concatenate | solution.py:213
  208.9 7.7 %fusion.13 = bf16[1024,1024]{1,0:T(8,128)(2,1)S(1)} fusion(bf16[2048,4096]{1,0:T(8,128)(2,1)S(1)} %pad_maximum_fusion, s32[]{:T(128)S(6)} %select_n.145, bf16[1024,1024]{0,1:T(8,128)(2,1)} %collective-permute-done.19, bf16[512,1024]{0,1:T(8,128)(2,1)S(1)} %copy-done.11, bf16[512,1024]{0,1:T(8,128)(2,1)S(1)} %copy-done.10), kind=kOutput, calls=%fused_computation.30 | convolution fusion | flops 4308598784 | bytes 10485764 | tf_op jit(solution)/shard_map/dot_general | solution.py:219
  218.2 6.2 %fusion.16 = bf16[1024,1024]{1,0:T(8,128)(2,1)S(1)} fusion(bf16[2048,4096]{1,0:T(8,128)(2,1)S(1)} %pad_maximum_fusion, s32[]{:T(128)S(6)} %select_n.146, bf16[1024,1024]{0,1:T(8,128)(2,1)} %collective-permute-done.19, bf16[512,1024]{0,1:T(8,128)(2,1)S(1)} %copy-done.11, bf16[512,1024]{0,1:T(8,128)(2,1)S(1)} %copy-done.10), kind=kOutput, calls=%fused_computation.31 | convolution fusion | flops 4308598784 | bytes 10485764 | tf_op jit(solution)/shard_map/dot_general | solution.py:219
  226.1 6.1 %fusion.10 = bf16[1024,1024]{1,0:T(8,128)(2,1)S(1)} fusion(bf16[2048,4096]{1,0:T(8,128)(2,1)S(1)} %pad_maximum_fusion, s32[]{:T(128)S(6)} %select_n.144, bf16[1024,1024]{0,1:T(8,128)(2,1)} %collective-permute-done.19, bf16[512,1024]{0,1:T(8,128)(2,1)S(1)} %copy-done.12, bf16[512,1024]{0,1:T(8,128)(2,1)S(1)} %copy-done.10), kind=kOutput, calls=%fused_computation.29 | convolution fusion | flops 4308598784 | bytes 10485764 | tf_op jit(solution)/shard_map/dot_general | solution.py:219
  234.3 5.9 %collective-permute-done.20 = bf16[512,1024]{1,0:T(8,128)(2,1)} collective-permute-done((bf16[512,1024]{1,0:T(8,128)(2,1)}, bf16[512,1024]{1,0:T(8,128)(2,1)}, u32[]{:S(2)}, u32[]{:S(2)}) %collective-permute-start.20) | collective-permute-done | bytes 1048608 | tf_op jit(solution)/shard_map/ppermute | solution.py:25
  243.8 7.9 %fusion.8 = bf16[1024,1024]{1,0:T(8,128)(2,1)S(1)} fusion(bf16[2048,4096]{1,0:T(8,128)(2,1)} %copy-done.5, s32[]{:T(128)S(6)} %select_n.142, bf16[1024,1024]{0,1:T(8,128)(2,1)} %collective-permute-done.19, bf16[512,1024]{0,1:T(8,128)(2,1)} %get-tuple-element.22, bf16[512,1024]{0,1:T(8,128)(2,1)} %get-tuple-element.20), kind=kOutput, calls=%fused_computation.18 | convolution fusion | flops 4307550208 | bytes 10485764 | tf_op jit(solution)/shard_map/dot_general | solution.py:219
  251.8 6.6 %collective-permute-done.23 = bf16[1024,1024]{1,0:T(8,128)(2,1)} collective-permute-done((bf16[1024,1024]{1,0:T(8,128)(2,1)S(1)}, bf16[1024,1024]{1,0:T(8,128)(2,1)}, u32[]{:S(2)}, u32[]{:S(2)}) %collective-permute-start.23) | collective-permute-done | bytes 2097184 | tf_op jit(solution)/shard_map/ppermute | solution.py:25
  258.4 12.0 %collective-permute-done.21 = bf16[1024,1024]{1,0:T(8,128)(2,1)} collective-permute-done((bf16[1024,1024]{1,0:T(8,128)(2,1)}, bf16[1024,1024]{1,0:T(8,128)(2,1)}, u32[]{:S(2)}, u32[]{:S(2)}) %collective-permute-start.21) | collective-permute-done | bytes 2097184 | tf_op jit(solution)/shard_map/ppermute | solution.py:25
  270.4 3.7 %add_convert_fusion = bf16[1024,1024]{1,0:T(8,128)(2,1)S(1)} fusion(bf16[1024,1024]{1,0:T(8,128)(2,1)} %collective-permute-done.23, bf16[1024,1024]{1,0:T(8,128)(2,1)} %collective-permute-done.21, bf16[1024,1024]{1,0:T(8,128)(2,1)S(1)} %fusion.8), kind=kLoop, calls=%fused_computation.7 | loop fusion | flops 6291456 | bytes 8388608 | tf_op jit(solution)/shard_map/convert_element_type | solution.py:223
  276.9 4.1 %collective-permute-done.24 = bf16[128,1024]{1,0:T(8,128)(2,1)S(1)} collective-permute-done((bf16[128,1024]{1,0:T(8,128)(2,1)S(1)}, bf16[128,1024]{1,0:T(8,128)(2,1)S(1)}, u32[]{:S(2)}, u32[]{:S(2)}) %collective-permute-start.24) | collective-permute-done | bytes 262176 | tf_op jit(solution)/shard_map/ppermute | solution.py:31
  286.3 5.6 %collective-permute-done.27 = bf16[256,1024]{1,0:T(8,128)(2,1)} collective-permute-done((bf16[256,1024]{1,0:T(8,128)(2,1)}, bf16[256,1024]{1,0:T(8,128)(2,1)}, u32[]{:S(2)}, u32[]{:S(2)}) %collective-permute-start.27) | collective-permute-done | bytes 524320 | tf_op jit(solution)/shard_map/ppermute | solution.py:31
  291.9 4.1 %collective-permute-done.25 = bf16[256,1024]{1,0:T(8,128)(2,1)S(1)} collective-permute-done((bf16[256,1024]{1,0:T(8,128)(2,1)}, bf16[256,1024]{1,0:T(8,128)(2,1)S(1)}, u32[]{:S(2)}, u32[]{:S(2)}) %collective-permute-start.25) | collective-permute-done | bytes 524320 | tf_op jit(solution)/shard_map/ppermute | solution.py:31
  314.9 2.7 collective-permute-start.35
  323.1 7.3 %collective-permute-done.37 = bf16[1024,256]{1,0:T(8,128)(2,1)S(1)} collective-permute-done((bf16[1024,256]{1,0:T(8,128)(2,1)S(1)}, bf16[1024,256]{1,0:T(8,128)(2,1)S(1)}, u32[]{:S(2)}, u32[]{:S(2)}) %collective-permute-start.37) | collective-permute-done | bytes 524320 | tf_op jit(solution)/shard_map/ppermute | solution.py:25
  330.5 2.7 collective-permute-start.39
  334.1 3.1 collective-permute-done.38
  345.1 12.3 %collective-permute-start.40 = (bf16[4096,256]{1,0:T(8,128)(2,1)S(1)}, bf16[4096,256]{1,0:T(8,128)(2,1)}, u32[]{:S(2)}, u32[]{:S(2)}) collective-permute-start(bf16[4096,256]{1,0:T(8,128)(2,1)S(1)} %constant_dynamic-slice_fusion.2), channel_id=1, source_target_pairs={{0,4},{4,0},{8,12},{12,8},{16,20},{20,16},{24,28},{28,24},{32,36},... | collective-permute-start | bytes 6291464 | tf_op jit(solution)/shard_map/ppermute | solution.py:41
  358.0 3.3 collective-permute-done.40
  361.4 4.7 %maximum_select_fusion = bf16[4096,512]{1,0:T(8,128)(2,1)} fusion(bf16[4096,256]{1,0:T(8,128)(2,1)} %collective-permute-done.40, bf16[4096,256]{1,0:T(8,128)(2,1)S(1)} %constant_dynamic-slice_fusion.2, pred[]{:T(512)S(6)} %eq.117), kind=kLoop, calls=%fused_computation.6 | loop fusion | flops 18874368 | bytes 8388609 | tf_op jit(solution)/shard_map/jit(_where)/select_n | solution.py:235
  (198 shorter events, 97.9 us)
Async XLA Ops:
  2.5 50.1 %collective-permute-start.1 = (bf16[4096,256]{1,0:T(8,128)(2,1)S(1)}, bf16[4096,256]{1,0:T(8,128)(2,1)}, u32[]{:S(2)}, u32[]{:S(2)}) collective-permute-start(bf16[4096,256]{1,0:T(8,128)(2,1)S(1)} %constant_dynamic-slice_fusion.6), channel_id=1, source_target_pairs={{0,1},{1,2},{2,3},{3,0},{4,5},{5,6},{6,7},{7,4},{8,9},{9,10},{10,1... | collective-permute-start | bytes 6291464 | tf_op jit(solution)/shard_map/ppermute | solution.py:37
  5.0 49.9 %collective-permute-start = (bf16[4096,256]{1,0:T(8,128)(2,1)S(1)}, bf16[4096,256]{1,0:T(8,128)(2,1)}, u32[]{:S(2)}, u32[]{:S(2)}) collective-permute-start(bf16[4096,256]{1,0:T(8,128)(2,1)S(1)} %constant_dynamic-slice_fusion.6), channel_id=1, source_target_pairs={{0,3},{1,0},{2,1},{3,2},{4,7},{5,4},{6,5},{7,6},{8,11},{9,8},{10,9... | collective-permute-start | bytes 6291464 | tf_op jit(solution)/shard_map/ppermute | solution.py:37
  15.7 78.1 %all-to-all-start = ((bf16[32,16,4224]{2,1,0:T(8,128)(2,1)}), bf16[32,16,4224]{2,1,0:T(8,128)(2,1)}, u32[]{:S(2)}, u32[]{:S(2)}) async-start(bf16[32,16,4224]{2,1,0:T(8,128)(2,1)} %bitcast.79), calls=%async_computation | async-start | bytes 8650752 | tf_op jit(solution)/shard_map/all_to_all | solution.py:145
  54.9 24.8 %collective-permute-start.2 = (bf16[2048,256]{1,0:T(8,128)(2,1)}, bf16[2048,256]{1,0:T(8,128)(2,1)S(1)}, u32[]{:S(2)}, u32[]{:S(2)}) collective-permute-start(bf16[2048,256]{1,0:T(8,128)(2,1)} %slice.175), channel_id=1, source_target_pairs={{0,1},{1,2},{2,3},{3,0},{4,5},{5,6},{6,7},{7,4},{8,9},{9,10},{10,1... | collective-permute-start | bytes 3145736 | tf_op jit(solution)/shard_map/ppermute | solution.py:37
  56.2 8.8 %copy-start.6 = (bf16[512,4096]{1,0:T(8,128)(2,1)S(1)}, bf16[512,4096]{1,0:T(8,128)(2,1)}, u32[]{:S(2)}) copy-start(bf16[512,4096]{1,0:T(8,128)(2,1)} %param.6) | copy-start | bytes 12582916
  56.2 24.6 %collective-permute-start.3 = (bf16[2048,256]{1,0:T(8,128)(2,1)S(1)}, bf16[2048,256]{1,0:T(8,128)(2,1)S(1)}, u32[]{:S(2)}, u32[]{:S(2)}) collective-permute-start(bf16[2048,256]{1,0:T(8,128)(2,1)S(1)} %slice.176), channel_id=1, source_target_pairs={{0,3},{1,0},{2,1},{3,2},{4,7},{5,4},{6,5},{7,6},{8,11},{9,8},{10,9... | collective-permute-start | bytes 3145736 | tf_op jit(solution)/shard_map/ppermute | solution.py:37
  63.3 68.8 %collective-permute-start.6 = (bf16[4096,256]{1,0:T(8,128)(2,1)}, bf16[4096,256]{1,0:T(8,128)(2,1)}, u32[]{:S(2)}, u32[]{:S(2)}) collective-permute-start(bf16[4096,256]{1,0:T(8,128)(2,1)} %collective-permute-done.1), channel_id=1, source_target_pairs={{0,4},{4,0},{8,12},{12,8},{16,20},{20,16},{24,28},{28,24},{32,36},... | collective-permute-start | bytes 6291464 | tf_op jit(solution)/shard_map/ppermute | solution.py:41
  65.0 54.6 %collective-permute-start.4 = (bf16[4096,256]{1,0:T(8,128)(2,1)}, bf16[4096,256]{1,0:T(8,128)(2,1)}, u32[]{:S(2)}, u32[]{:S(2)}) collective-permute-start(bf16[4096,256]{1,0:T(8,128)(2,1)} %collective-permute-done), channel_id=1, source_target_pairs={{0,4},{4,0},{8,12},{12,8},{16,20},{20,16},{24,28},{28,24},{32,36},... | collective-permute-start | bytes 6291464 | tf_op jit(solution)/shard_map/ppermute | solution.py:41
  81.9 46.0 %collective-permute-start.5 = (bf16[4096,256]{1,0:T(8,128)(2,1)}, bf16[4096,256]{1,0:T(8,128)(2,1)}, u32[]{:S(2)}, u32[]{:S(2)}) collective-permute-start(bf16[4096,256]{1,0:T(8,128)(2,1)} %constant_dynamic-update-slice_fusion), channel_id=1, source_target_pairs={{0,4},{4,0},{8,12},{12,8},{16,20},{20,16},{24,28},{28,24},{32,36},... | collective-permute-start | bytes 6291464 | tf_op jit(solution)/shard_map/ppermute | solution.py:41
  136.2 11.5 %copy-start.3 = (f32[512,2048]{0,1:T(8,128)}, f32[512,2048]{0,1:T(8,128)S(1)}, u32[]{:S(2)}) copy-start(f32[512,2048]{0,1:T(8,128)S(1)} %convolution_dynamic-update-slice_fusion) | copy-start | bytes 12582916
  152.2 4.4 %collective-permute-start.9 = (f32[64,128]{1,0:T(8,128)S(1)}, f32[64,128]{1,0:T(8,128)S(1)}, u32[]{:S(2)}, u32[]{:S(2)}) collective-permute-start(f32[64,128]{1,0:T(8,128)S(1)} %copy.58), channel_id=1, source_target_pairs={{0,64},{4,20},{8,72},{12,28},{16,80},{20,4},{24,88},{28,12},{32,96... | collective-permute-start | bytes 98312 | tf_op jit(solution)/shard_map/ppermute | solution.py:25
  155.2 2.8 collective-permute-start.8
  156.0 4.0 %collective-permute-start.7 = (f32[64,128]{1,0:T(8,128)S(1)}, f32[64,128]{1,0:T(8,128)S(1)}, u32[]{:S(2)}, u32[]{:S(2)}) collective-permute-start(f32[64,128]{1,0:T(8,128)S(1)} %copy.58), channel_id=1, source_target_pairs={{0,32},{4,12},{8,40},{12,20},{16,48},{20,28},{24,56},{28,4},{32,64... | collective-permute-start | bytes 98312 | tf_op jit(solution)/shard_map/ppermute | solution.py:25
  159.9 4.3 %collective-permute-start.12 = (f32[64,128]{1,0:T(8,128)S(1)}, f32[64,128]{1,0:T(8,128)S(1)}, u32[]{:S(2)}, u32[]{:S(2)}) collective-permute-start(f32[64,128]{1,0:T(8,128)S(1)} %add_add_fusion.2), channel_id=1, source_target_pairs={{0,16},{4,68},{8,24},{12,76},{16,0},{20,84},{24,8},{28,92},{32,48}... | collective-permute-start | bytes 98312 | tf_op jit(solution)/shard_map/ppermute | solution.py:31
  162.8 3.1 collective-permute-start.11
  163.6 4.0 %collective-permute-start.10 = (f32[64,128]{1,0:T(8,128)S(1)}, f32[64,128]{1,0:T(8,128)S(1)}, u32[]{:S(2)}, u32[]{:S(2)}) collective-permute-start(f32[64,128]{1,0:T(8,128)S(1)} %add_add_fusion.2), channel_id=1, source_target_pairs={{0,8},{4,36},{8,16},{12,44},{16,24},{20,52},{24,0},{28,60},{32,40}... | collective-permute-start | bytes 98312 | tf_op jit(solution)/shard_map/ppermute | solution.py:31
  167.6 4.4 %collective-permute-start.13 = (f32[64,128]{1,0:T(8,128)S(1)}, f32[64,128]{1,0:T(8,128)S(1)}, u32[]{:S(2)}, u32[]{:S(2)}) collective-permute-start(f32[64,128]{1,0:T(8,128)S(1)} %add_add_fusion.1), channel_id=1, source_target_pairs={{0,4},{4,0},{8,12},{12,8},{16,20},{20,16},{24,28},{28,24},{32,36},... | collective-permute-start | bytes 98312 | tf_op jit(solution)/shard_map/ppermute | solution.py:41
  172.0 9.4 %collective-permute-start.16 = (f32[64,128]{1,0:T(8,128)S(1)}, f32[64,128]{1,0:T(8,128)S(1)}, u32[]{:S(2)}, u32[]{:S(2)}) collective-permute-start(f32[64,128]{1,0:T(8,128)S(1)} %add.191), channel_id=1, source_target_pairs={{0,2},{1,3},{2,0},{3,1},{4,6},{5,7},{6,4},{7,5},{8,10},{9,11},{10,... | collective-permute-start | bytes 98312 | tf_op jit(solution)/shard_map/ppermute | solution.py:37
  173.3 8.1 %collective-permute-start.15 = (f32[64,128]{1,0:T(8,128)S(1)}, f32[64,128]{1,0:T(8,128)S(1)}, u32[]{:S(2)}, u32[]{:S(2)}) collective-permute-start(f32[64,128]{1,0:T(8,128)S(1)} %add.191), channel_id=1, source_target_pairs={{0,3},{1,0},{2,1},{3,2},{4,7},{5,4},{6,5},{7,6},{8,11},{9,8},{10,9... | collective-permute-start | bytes 98312 | tf_op jit(solution)/shard_map/ppermute | solution.py:37
  174.8 6.6 %collective-permute-start.14 = (f32[64,128]{1,0:T(8,128)S(1)}, f32[64,128]{1,0:T(8,128)S(1)}, u32[]{:S(2)}, u32[]{:S(2)}) collective-permute-start(f32[64,128]{1,0:T(8,128)S(1)} %add.191), channel_id=1, source_target_pairs={{0,1},{1,2},{2,3},{3,0},{4,5},{5,6},{6,7},{7,4},{8,9},{9,10},{10,1... | collective-permute-start | bytes 98312 | tf_op jit(solution)/shard_map/ppermute | solution.py:37
  175.4 24.8 %collective-permute-start.17 = (bf16[512,4096]{1,0:T(8,128)(2,1)}, bf16[512,4096]{1,0:T(8,128)(2,1)}, u32[]{:S(2)}, u32[]{:S(2)}) collective-permute-start(bf16[512,4096]{1,0:T(8,128)(2,1)} %param.6), channel_id=1, source_target_pairs={{0,4},{4,0},{8,12},{12,8},{16,20},{20,16},{24,28},{28,24},{32,36},... | collective-permute-start | bytes 12582920 | tf_op jit(solution)/shard_map/ppermute | solution.py:41
  181.4 18.8 %collective-permute-start.18 = (bf16[512,4096]{1,0:T(8,128)(2,1)}, bf16[512,4096]{1,0:T(8,128)(2,1)}, u32[]{:S(2)}, u32[]{:S(2)}) collective-permute-start(bf16[512,4096]{1,0:T(8,128)(2,1)} %slice.174), channel_id=1, source_target_pairs={{0,4},{4,0},{8,12},{12,8},{16,20},{20,16},{24,28},{28,24},{32,36},... | collective-permute-start | bytes 12582920 | tf_op jit(solution)/shard_map/ppermute | solution.py:41
  199.4 9.5 %collective-permute-start.19 = (bf16[1024,1024]{0,1:T(8,128)(2,1)S(1)}, bf16[1024,1024]{0,1:T(8,128)(2,1)}, u32[]{:S(2)}, u32[]{:S(2)}) collective-permute-start(bf16[1024,1024]{0,1:T(8,128)(2,1)S(1)} %pad_maximum_fusion.2), channel_id=1, source_target_pairs={{0,4},{4,0},{8,12},{12,8},{16,20},{20,16},{24,28},{28,24},{32,36},... | collective-permute-start | bytes 6291464 | tf_op jit(solution)/shard_map/ppermute | solution.py:41
  200.2 8.7 %copy-start.10 = (bf16[512,1024]{0,1:T(8,128)(2,1)S(1)}, bf16[512,1024]{0,1:T(8,128)(2,1)}, u32[]{:S(2)}) copy-start(bf16[512,1024]{0,1:T(8,128)(2,1)} %get-tuple-element.20) | copy-start | bytes 3145732
  200.2 8.7 %copy-start.11 = (bf16[512,1024]{0,1:T(8,128)(2,1)S(1)}, bf16[512,1024]{0,1:T(8,128)(2,1)}, u32[]{:S(2)}) copy-start(bf16[512,1024]{0,1:T(8,128)(2,1)} %get-tuple-element.22) | copy-start | bytes 3145732
  208.9 17.3 %copy-start.5 = (bf16[2048,4096]{1,0:T(8,128)(2,1)}, bf16[2048,4096]{1,0:T(8,128)(2,1)S(1)}, u32[]{:S(2)}) copy-start(bf16[2048,4096]{1,0:T(8,128)(2,1)S(1)} %pad_maximum_fusion) | copy-start | bytes 50331652
  218.2 14.3 %collective-permute-start.22 = (bf16[512,1024]{1,0:T(8,128)(2,1)}, bf16[512,1024]{1,0:T(8,128)(2,1)S(1)}, u32[]{:S(2)}, u32[]{:S(2)}) collective-permute-start(bf16[512,1024]{1,0:T(8,128)(2,1)} %get-tuple-element.19), channel_id=1, source_target_pairs={{0,96},{4,28},{8,104},{12,4},{16,112},{20,12},{24,120},{28,20},{32... | collective-permute-start | bytes 3145736 | tf_op jit(solution)/shard_map/ppermute | solution.py:25
  224.5 15.8 %collective-permute-start.20 = (bf16[512,1024]{1,0:T(8,128)(2,1)}, bf16[512,1024]{1,0:T(8,128)(2,1)}, u32[]{:S(2)}, u32[]{:S(2)}) collective-permute-start(bf16[512,1024]{1,0:T(8,128)(2,1)} %get-tuple-element.18), channel_id=1, source_target_pairs={{0,32},{4,12},{8,40},{12,20},{16,48},{20,28},{24,56},{28,4},{32,64... | collective-permute-start | bytes 3145736 | tf_op jit(solution)/shard_map/ppermute | solution.py:25
  233.0 25.4 %collective-permute-start.23 = (bf16[1024,1024]{1,0:T(8,128)(2,1)S(1)}, bf16[1024,1024]{1,0:T(8,128)(2,1)}, u32[]{:S(2)}, u32[]{:S(2)}) collective-permute-start(bf16[1024,1024]{1,0:T(8,128)(2,1)S(1)} %pad_maximum_fusion.4), channel_id=1, source_target_pairs={{0,96},{4,28},{8,104},{12,4},{16,112},{20,12},{24,120},{28,20},{32... | collective-permute-start | bytes 6291464 | tf_op jit(solution)/shard_map/ppermute | solution.py:25
  243.4 26.9 %collective-permute-start.21 = (bf16[1024,1024]{1,0:T(8,128)(2,1)}, bf16[1024,1024]{1,0:T(8,128)(2,1)}, u32[]{:S(2)}, u32[]{:S(2)}) collective-permute-start(bf16[1024,1024]{1,0:T(8,128)(2,1)} %pad_maximum_fusion.3), channel_id=1, source_target_pairs={{0,32},{4,12},{8,40},{12,20},{16,48},{20,28},{24,56},{28,4},{32,64... | collective-permute-start | bytes 6291464 | tf_op jit(solution)/shard_map/ppermute | solution.py:25
  274.2 6.8 %collective-permute-start.24 = (bf16[128,1024]{1,0:T(8,128)(2,1)S(1)}, bf16[128,1024]{1,0:T(8,128)(2,1)S(1)}, u32[]{:S(2)}, u32[]{:S(2)}) collective-permute-start(bf16[128,1024]{1,0:T(8,128)(2,1)S(1)} %get-tuple-element.14), channel_id=1, source_target_pairs={{0,8},{4,36},{8,16},{12,44},{16,24},{20,52},{24,0},{28,60},{32,40}... | collective-permute-start | bytes 786440 | tf_op jit(solution)/shard_map/ppermute | solution.py:31
  274.3 6.7 %collective-permute-start.26 = (bf16[128,1024]{1,0:T(8,128)(2,1)S(1)}, bf16[128,1024]{1,0:T(8,128)(2,1)}, u32[]{:S(2)}, u32[]{:S(2)}) collective-permute-start(bf16[128,1024]{1,0:T(8,128)(2,1)S(1)} %get-tuple-element.16), channel_id=1, source_target_pairs={{0,24},{4,100},{8,0},{12,108},{16,8},{20,116},{24,16},{28,124},{32... | collective-permute-start | bytes 786440 | tf_op jit(solution)/shard_map/ppermute | solution.py:31
  282.9 8.9 %collective-permute-start.27 = (bf16[256,1024]{1,0:T(8,128)(2,1)}, bf16[256,1024]{1,0:T(8,128)(2,1)}, u32[]{:S(2)}, u32[]{:S(2)}) collective-permute-start(bf16[256,1024]{1,0:T(8,128)(2,1)} %pad_maximum_fusion.6), channel_id=1, source_target_pairs={{0,24},{4,100},{8,0},{12,108},{16,8},{20,116},{24,16},{28,124},{32... | collective-permute-start | bytes 1572872 | tf_op jit(solution)/shard_map/ppermute | solution.py:31
  286.3 9.7 %collective-permute-start.25 = (bf16[256,1024]{1,0:T(8,128)(2,1)}, bf16[256,1024]{1,0:T(8,128)(2,1)S(1)}, u32[]{:S(2)}, u32[]{:S(2)}) collective-permute-start(bf16[256,1024]{1,0:T(8,128)(2,1)} %pad_maximum_fusion.5), channel_id=1, source_target_pairs={{0,8},{4,36},{8,16},{12,44},{16,24},{20,52},{24,0},{28,60},{32,40}... | collective-permute-start | bytes 1572872 | tf_op jit(solution)/shard_map/ppermute | solution.py:31
  297.4 4.4 %collective-permute-start.28 = (bf16[128,256]{1,0:T(8,128)(2,1)S(1)}, bf16[128,256]{1,0:T(8,128)(2,1)S(1)}, u32[]{:S(2)}, u32[]{:S(2)}) collective-permute-start(bf16[128,256]{1,0:T(8,128)(2,1)S(1)} %get-tuple-element.26), channel_id=1, source_target_pairs={{0,1},{1,2},{2,3},{3,0},{4,5},{5,6},{6,7},{7,4},{8,9},{9,10},{10,1... | collective-permute-start | bytes 196616 | tf_op jit(solution)/shard_map/ppermute | solution.py:37
  299.2 3.1 collective-permute-start.30
  302.3 4.9 %collective-permute-start.31 = (bf16[256,256]{1,0:T(8,128)(2,1)S(1)}, bf16[256,256]{1,0:T(8,128)(2,1)S(1)}, u32[]{:S(2)}, u32[]{:S(2)}) collective-permute-start(bf16[256,256]{1,0:T(8,128)(2,1)S(1)} %pad_maximum_fusion.8), channel_id=1, source_target_pairs={{0,3},{1,0},{2,1},{3,2},{4,7},{5,4},{6,5},{7,6},{8,11},{9,8},{10,9... | collective-permute-start | bytes 393224 | tf_op jit(solution)/shard_map/ppermute | solution.py:37
  304.6 5.1 %collective-permute-start.29 = (bf16[256,256]{1,0:T(8,128)(2,1)S(1)}, bf16[256,256]{1,0:T(8,128)(2,1)S(1)}, u32[]{:S(2)}, u32[]{:S(2)}) collective-permute-start(bf16[256,256]{1,0:T(8,128)(2,1)S(1)} %pad_maximum_fusion.7), channel_id=1, source_target_pairs={{0,1},{1,2},{2,3},{3,0},{4,5},{5,6},{6,7},{7,4},{8,9},{9,10},{10,1... | collective-permute-start | bytes 393224 | tf_op jit(solution)/shard_map/ppermute | solution.py:37
  309.7 5.1 %collective-permute-start.33 = (bf16[256,256]{1,0:T(8,128)(2,1)S(1)}, bf16[256,256]{1,0:T(8,128)(2,1)S(1)}, u32[]{:S(2)}, u32[]{:S(2)}) collective-permute-start(bf16[256,256]{1,0:T(8,128)(2,1)S(1)} %get-tuple-element.9), channel_id=1, source_target_pairs={{0,8},{4,36},{8,16},{12,44},{16,24},{20,52},{24,0},{28,60},{32,40}... | collective-permute-start | bytes 393224 | tf_op jit(solution)/shard_map/ppermute | solution.py:31
  309.8 5.0 %collective-permute-start.32 = (bf16[256,256]{1,0:T(8,128)(2,1)S(1)}, bf16[256,256]{1,0:T(8,128)(2,1)S(1)}, u32[]{:S(2)}, u32[]{:S(2)}) collective-permute-start(bf16[256,256]{1,0:T(8,128)(2,1)S(1)} %get-tuple-element.9), channel_id=1, source_target_pairs={{0,24},{4,100},{8,0},{12,108},{16,8},{20,116},{24,16},{28,124},{32... | collective-permute-start | bytes 393224 | tf_op jit(solution)/shard_map/ppermute | solution.py:31
  314.8 4.3 %collective-permute-start.34 = (bf16[128,256]{1,0:T(8,128)(2,1)S(1)}, bf16[128,256]{1,0:T(8,128)(2,1)S(1)}, u32[]{:S(2)}, u32[]{:S(2)}) collective-permute-start(bf16[128,256]{1,0:T(8,128)(2,1)S(1)} %slice.200), channel_id=1, source_target_pairs={{0,8},{4,36},{8,16},{12,44},{16,24},{20,52},{24,0},{28,60},{32,40}... | collective-permute-start | bytes 196616 | tf_op jit(solution)/shard_map/ppermute | solution.py:31
  314.9 4.3 %collective-permute-start.35 = (bf16[128,256]{1,0:T(8,128)(2,1)S(1)}, bf16[128,256]{1,0:T(8,128)(2,1)S(1)}, u32[]{:S(2)}, u32[]{:S(2)}) collective-permute-start(bf16[128,256]{1,0:T(8,128)(2,1)S(1)} %slice.201), channel_id=1, source_target_pairs={{0,24},{4,100},{8,0},{12,108},{16,8},{20,116},{24,16},{28,124},{32... | collective-permute-start | bytes 196616 | tf_op jit(solution)/shard_map/ppermute | solution.py:31
  320.2 10.2 %collective-permute-start.37 = (bf16[1024,256]{1,0:T(8,128)(2,1)S(1)}, bf16[1024,256]{1,0:T(8,128)(2,1)S(1)}, u32[]{:S(2)}, u32[]{:S(2)}) collective-permute-start(bf16[1024,256]{1,0:T(8,128)(2,1)S(1)} %get-tuple-element.7), channel_id=1, source_target_pairs={{0,32},{4,12},{8,40},{12,20},{16,48},{20,28},{24,56},{28,4},{32,64... | collective-permute-start | bytes 1572872 | tf_op jit(solution)/shard_map/ppermute | solution.py:25
  320.4 10.0 %collective-permute-start.36 = (bf16[1024,256]{1,0:T(8,128)(2,1)S(1)}, bf16[1024,256]{1,0:T(8,128)(2,1)S(1)}, u32[]{:S(2)}, u32[]{:S(2)}) collective-permute-start(bf16[1024,256]{1,0:T(8,128)(2,1)S(1)} %get-tuple-element.7), channel_id=1, source_target_pairs={{0,96},{4,28},{8,104},{12,4},{16,112},{20,12},{24,120},{28,20},{32... | collective-permute-start | bytes 1572872 | tf_op jit(solution)/shard_map/ppermute | solution.py:25
  330.4 6.8 %collective-permute-start.38 = (bf16[512,256]{1,0:T(8,128)(2,1)S(1)}, bf16[512,256]{1,0:T(8,128)(2,1)S(1)}, u32[]{:S(2)}, u32[]{:S(2)}) collective-permute-start(bf16[512,256]{1,0:T(8,128)(2,1)S(1)} %slice.202), channel_id=1, source_target_pairs={{0,32},{4,12},{8,40},{12,20},{16,48},{20,28},{24,56},{28,4},{32,64... | collective-permute-start | bytes 786440 | tf_op jit(solution)/shard_map/ppermute | solution.py:25
  330.5 7.4 %collective-permute-start.39 = (bf16[512,256]{1,0:T(8,128)(2,1)S(1)}, bf16[512,256]{1,0:T(8,128)(2,1)S(1)}, u32[]{:S(2)}, u32[]{:S(2)}) collective-permute-start(bf16[512,256]{1,0:T(8,128)(2,1)S(1)} %slice.203), channel_id=1, source_target_pairs={{0,96},{4,28},{8,104},{12,4},{16,112},{20,12},{24,120},{28,20},{32... | collective-permute-start | bytes 786440 | tf_op jit(solution)/shard_map/ppermute | solution.py:25
  345.1 16.3 %collective-permute-start.40 = (bf16[4096,256]{1,0:T(8,128)(2,1)S(1)}, bf16[4096,256]{1,0:T(8,128)(2,1)}, u32[]{:S(2)}, u32[]{:S(2)}) collective-permute-start(bf16[4096,256]{1,0:T(8,128)(2,1)S(1)} %constant_dynamic-slice_fusion.2), channel_id=1, source_target_pairs={{0,4},{4,0},{8,12},{12,8},{16,20},{20,16},{24,28},{28,24},{32,36},... | collective-permute-start | bytes 6291464 | tf_op jit(solution)/shard_map/ppermute | solution.py:41
  357.5 8.6 %copy-start.1 = (bf16[128,4096]{1,0:T(8,128)(2,1)S(1)}, bf16[128,4096]{1,0:T(8,128)(2,1)}, u32[]{:S(2)}) copy-start(bf16[128,4096]{1,0:T(8,128)(2,1)} %param.5) | copy-start | bytes 3145732
  (9 other events, 48.8 us)

commit v2 on v1

v2 whole, which is shorter than its diff:
```python
import functools

import jax
import jax.numpy as jnp
from jax import lax
from jax.experimental import pallas as pl
from jax.experimental.pallas import tpu as pltpu
from jax.sharding import PartitionSpec as P

CAP = 2
INV_TAU = 50.0
F32 = jnp.float32
BF16 = jnp.bfloat16
SIDE = 4
VMEM = 48 * 2**20


def dp_perm(move):
    pairs = []
    for x in range(SIDE):
        for y in range(SIDE):
            for core in range(2):
                tx, ty, tcore = move(x, y, core)
                target = ((tx % SIDE) * SIDE + ty % SIDE) * 2 + tcore
                pairs.append(((x * SIDE + y) * 2 + core, target))
    return pairs


def first(value, step):
    return lax.ppermute(
        value, "dp", dp_perm(lambda x, y, k: (x + step, y, k) if k == 0 else (x, y + step, k))
    )


def second(value, step):
    return lax.ppermute(
        value, "dp", dp_perm(lambda x, y, k: (x, y + step, k) if k == 0 else (x + step, y, k))
    )


def third(value, step):
    return lax.ppermute(value, "psg", [(c, (c + step) % SIDE) for c in range(SIDE)])


def swap(value):
    return lax.ppermute(value, "dp", dp_perm(lambda x, y, k: (x, y, 1 - k)))


def ring_sum(value, move):
    return value + move(value, 1) + move(value, -1) + move(value, 2)


def dot(left, right, contract):
    return lax.dot_general(
        left, right, ((contract[:1], contract[1:]), ((), ())), preferred_element_type=F32
    )


def cost(flops, nbytes, exps=0):
    return pl.CostEstimate(flops=flops, bytes_accessed=nbytes, transcendentals=exps)


def project_kernel(pt, pb, qt, qb, mt, mb, tt, tb, out):
    first_step = pl.program_id(0) == 0
    rows = pt.shape[0]
    half = mt.shape[1]
    for row, (top, bottom) in enumerate(((pt, pb), (qt, qb))):
        for col, (wt, wb) in enumerate(((mt, mb), (tt, tb))):
            value = dot(top[...], wt[...], (1, 0)) + dot(bottom[...], wb[...], (1, 0))
            where = (pl.ds(row * rows, rows), pl.ds(col * half, half))

            @pl.when(first_step)
            def _():
                out[where] = value

            @pl.when(jnp.logical_not(first_step))
            def _():
                out[where] += value


def project(states, asked, mine, theirs):
    rows, depth = states.shape
    half = mine[0].shape[1]
    steps = SIDE
    tile = depth // 2 // steps
    top = pl.BlockSpec((rows, tile), lambda i: (0, i))
    bottom = pl.BlockSpec((rows, tile), lambda i: (0, i + steps))
    weight = pl.BlockSpec((tile, half), lambda i: (i, 0))
    return pl.pallas_call(
        project_kernel,
        grid=(steps,),
        in_specs=[top, bottom, top, bottom] + [weight] * 4,
        out_specs=pl.BlockSpec((2 * rows, 2 * half), lambda i: (0, 0)),
        out_shape=jax.ShapeDtypeStruct((2 * rows, 2 * half), F32),
        compiler_params=pltpu.CompilerParams(vmem_limit_bytes=VMEM),
        cost_estimate=cost(8 * rows * depth * half, 4 * rows * depth + 4 * depth * half + 16 * rows * half),
        name="project",
    )(states, states, asked, asked, mine[0], mine[1], theirs[0], theirs[1])


def score_kernel(r0, r1, r2, r3, chosen, valid, emb, exps, scale_out, sums, hits):
    step = pl.program_id(0)
    tile = r0.shape[0]
    width = r0.shape[1]
    rows = exps.shape[0]
    values = [r[...] for r in (r0, r1, r2, r3)]
    square = values[0] * values[0]
    for value in values[1:]:
        square = square + value * value
    scale = 1.0 / jnp.sqrt(jnp.sum(square, axis=1, keepdims=True) + 1e-06)
    scale_out[...] = scale
    for i, value in enumerate(values):
        emb[pl.ds(step * tile, tile), i * width : (i + 1) * width] = (value * scale).astype(BF16)

    @pl.when(step == pl.num_programs(0) - 1)
    def _():
        chunk = rows // SIDE
        queries = emb[rows:, :]
        total = jnp.zeros((1, queries.shape[0]), F32)
        found = jnp.zeros((1, queries.shape[0]), F32)
        for i in range(SIDE):
            part = dot(emb[i * chunk : (i + 1) * chunk, :], queries, (1, 1)) * INV_TAU
            place = lax.broadcasted_iota(jnp.int32, part.shape, 0) + i * chunk
            value = jnp.exp(part)
            exps[i * chunk : (i + 1) * chunk, :] = value
            total = total + jnp.sum(value, axis=0, keepdims=True)
            found = found + jnp.sum(
                jnp.where(place == chosen[...], part, 0.0), axis=0, keepdims=True
            )
        sums[...] = jnp.where(valid[...] == 1, total, 0.0)
        hits[...] = found


def score(raws, chosen, valid):
    both, width = raws[0].shape
    rows = both // 2
    steps = 8
    tile = both // steps
    features = width * SIDE
    raw = pl.BlockSpec((tile, width), lambda i: (i, 0))
    line = pl.BlockSpec((1, rows), lambda i: (0, 0))
    return pl.pallas_call(
        score_kernel,
        grid=(steps,),
        in_specs=[raw] * SIDE + [line] * 2,
        out_specs=[
            pl.BlockSpec((both, features), lambda i: (0, 0)),
            pl.BlockSpec((rows, rows), lambda i: (0, 0)),
            pl.BlockSpec((tile, 1), lambda i: (i, 0)),
            line,
            line,
        ],
        out_shape=[
            jax.ShapeDtypeStruct((both, features), BF16),
            jax.ShapeDtypeStruct((rows, rows), F32),
            jax.ShapeDtypeStruct((both, 1), F32),
            jax.ShapeDtypeStruct((1, rows), F32),
            jax.ShapeDtypeStruct((1, rows), F32),
        ],
        compiler_params=pltpu.CompilerParams(vmem_limit_bytes=VMEM),
        cost_estimate=cost(2 * rows * rows * features, 6 * both * features + 4 * rows * rows, rows * rows),
        name="score",
    )(*raws, chosen, valid)


def backward_kernel(emb, exps, scale, denom, chosen, mine, theirs, grads, d_emb):
    rows = exps.shape[0]
    features = emb.shape[1]
    width = features // SIDE
    half = width // 2
    inverse = 1.0 / denom[...]
    chunk = rows // SIDE
    for i in range(SIDE):
        where = slice(i * chunk, (i + 1) * chunk)
        place = lax.broadcasted_iota(jnp.int32, (chunk, rows), 0) + i * chunk
        target = jnp.where(place == chosen[...], 1.0, 0.0)
        grads[where, :] = (exps[where, :] * inverse - target).astype(BF16)
    for i in range(SIDE):
        cols = slice(i * width, (i + 1) * width)
        d_emb[:rows, cols] = dot(grads[...], emb[rows:, cols], (1, 0)) * INV_TAU
        d_emb[rows:, cols] = dot(grads[...], emb[:rows, cols], (0, 0)) * INV_TAU
    tile = 64

    @pl.loop(0, 2 * rows // tile)
    def _(step):
        where = pl.ds(pl.multiple_of(step * tile, tile), tile)
        inner = jnp.zeros((tile, 1), F32)
        for i in range(SIDE):
            cols = slice(i * width, (i + 1) * width)
            inner = inner + jnp.sum(
                emb[where, cols].astype(F32) * d_emb[where, cols], axis=1, keepdims=True
            )
        factor = scale[where, :]
        for i in range(SIDE):
            for j, out in enumerate((mine, theirs)):
                cols = slice(i * width + j * half, i * width + (j + 1) * half)
                out[where, i * half : (i + 1) * half] = (
                    (d_emb[where, cols] - emb[where, cols].astype(F32) * inner) * factor
                ).astype(BF16)


def backward(emb, exps, scale, denom, chosen):
    both, features = emb.shape
    rows = both // 2
    return pl.pallas_call(
        backward_kernel,
        out_shape=[jax.ShapeDtypeStruct((both, features // 2), BF16)] * 2,
        scratch_shapes=[pltpu.VMEM((rows, rows), BF16), pltpu.VMEM((both, features), F32)],
        compiler_params=pltpu.CompilerParams(vmem_limit_bytes=VMEM),
        cost_estimate=cost(4 * rows * rows * features, 4 * both * features + 4 * rows * rows),
        name="backward",
    )(emb, exps, scale, denom, chosen)


def weight_kernel(cols, p, q, op, oq, d, od, *outs):
    del cols
    step = pl.program_id(0)
    rows = p.shape[0]
    value = dot(p[...], d[:rows, :], (0, 0)) + dot(q[...], d[rows:, :], (0, 0))
    value = value + dot(op[...], od[:rows, :], (0, 0)) + dot(oq[...], od[rows:, :], (0, 0))
    value = value.astype(BF16)
    for i, out in enumerate(outs):

        @pl.when(step // 2 == i)
        def _():
            out[...] = value


def weight_terms(states, d_mine, d_other, u, items, part):
    rows = states[0].shape[0]
    tile = part // SIDE
    keep = d_mine.shape[1]
    cols = jnp.stack(
        [
            lax.rem(u + step, SIDE) * SIDE + part_half * 2 + t
            for step, part_half in items
            for t in range(2)
        ]
    ).astype(jnp.int32)
    state = pl.BlockSpec((rows, tile), lambda i, cols: (0, cols[i]))
    grad = pl.BlockSpec(d_mine.shape, lambda i, cols: (0, 0))
    outs = [
        pl.BlockSpec((tile, keep), lambda i, cols, j=j: (jnp.clip(i - 2 * j, 0, 1), 0))
        for j in range(len(items))
    ]
    grid_spec = pltpu.PrefetchScalarGridSpec(
        num_scalar_prefetch=1,
        grid=(2 * len(items),),
        in_specs=[state] * 4 + [grad] * 2,
        out_specs=outs,
    )
    return pl.pallas_call(
        weight_kernel,
        grid_spec=grid_spec,
        out_shape=[jax.ShapeDtypeStruct((2 * tile, keep), BF16)] * len(items),
        compiler_params=pltpu.CompilerParams(vmem_limit_bytes=VMEM),
        cost_estimate=cost(
            16 * rows * tile * keep * len(items),
            (16 * rows * tile + 4 * tile * keep) * len(items) + 8 * rows * keep,
        ),
        name="weight_terms",
    )(cols, *states, d_mine, d_other)


def place_kernel(places, *refs):
    *pieces, out, sems = refs
    count = len(pieces) // 2
    copies = []
    half = pieces[0].shape[1]
    core = places[2]
    for side in range(2):
        a = places[side]
        b = places[1 - side]
        col = pl.multiple_of(jnp.where(core == side, 0, half), half)
        for number in range(count):
            ref = pieces[side * count + number]
            rows = out.shape[0] // (SIDE * SIDE)
            for inner in range(ref.shape[0] // rows):
                far = (0, 1, 2, 2, 3)[number]
                rel = inner + (2 if number == 3 else 0)
                row = lax.rem(a + far, SIDE) * SIDE + lax.rem(b + rel, SIDE)
                copies.append(
                    pltpu.make_async_copy(
                        ref.at[pl.ds(inner * rows, rows), :],
                        out.at[pl.ds(pl.multiple_of(row * rows, rows), rows), pl.ds(col, half)],
                        sems.at[len(copies)],
                    )
                )
    for copy in copies:
        copy.start()
    for copy in copies:
        copy.wait()


def place_all(mine, other, u, v, core):
    total = SIDE * SIDE * (mine[0].shape[0] // SIDE)
    half = mine[0].shape[1]
    places = jnp.stack([u, v, core]).astype(jnp.int32)
    count = 2 * SIDE * SIDE
    return pl.pallas_call(
        place_kernel,
        in_specs=[pl.BlockSpec(memory_space=pltpu.SMEM)] + [pl.BlockSpec(memory_space=pl.ANY)] * 10,
        out_specs=pl.BlockSpec(memory_space=pl.ANY),
        out_shape=jax.ShapeDtypeStruct((total, 2 * half), BF16),
        scratch_shapes=[pltpu.SemaphoreType.DMA((count,))],
        name="place_all",
    )(places, *mine, *other)


def add(*values):
    total = values[0].astype(F32)
    for value in values[1:]:
        total = total + value.astype(F32)
    return total.astype(BF16)


def routes(mine, per_block, ranks):
    blocks, slots = mine.shape
    same = (mine[:, :, None, None] == mine[None, None, :, :]).astype(jnp.int32)
    before = (
        lax.broadcasted_iota(jnp.int32, (blocks, blocks), 1)
        < lax.broadcasted_iota(jnp.int32, (blocks, blocks), 0)
    ).astype(jnp.int32)
    place = jnp.sum(same * before[:, None, :, None], axis=(2, 3))
    line = mine * CAP + place
    rows = ranks * CAP * per_block
    line = jnp.repeat(line, per_block, axis=0)
    count = blocks * per_block
    row = lax.broadcasted_iota(jnp.int32, (rows, count), 0)
    col = lax.broadcasted_iota(jnp.int32, (rows, count), 1)
    aligned = lax.rem(row, per_block) == lax.rem(col, per_block)
    row_line = row // per_block
    hot = [aligned & (row_line == line[None, :, s]) for s in range(slots)]
    return (hot[0] | hot[1]).astype(BF16), hot[0].astype(BF16)


def shards(query_states, passage_last_states, head_weight, negatives, positives):
    ranks = lax.axis_size("dp")
    groups = lax.axis_size("psg")
    dp = lax.axis_index("dp")
    column = lax.axis_index("psg")
    core = lax.rem(dp, 2)
    x = dp // (2 * SIDE)
    y = lax.rem(dp // 2, SIDE)
    u = jnp.where(core == 0, x, y)
    v = jnp.where(core == 0, y, x)
    queries, depth = query_states.shape
    blocks = negatives.shape[1]
    per_block = queries // blocks
    share = head_weight.shape[1]
    half = share // 2
    deep = depth // 2

    def own(which, row):
        return lax.dynamic_slice(head_weight, (row * deep, which * half), (deep, half))

    mine0 = [own(core, 0), own(core, 1)]
    theirs0 = [own(1 - core, 0), own(1 - core, 1)]
    left_top = third(mine0[0], 1)
    right_bottom = third(mine0[1], -1)
    left_bottom = third(mine0[1], 1)
    right_top = third(mine0[0], -1)
    mine1 = [right_top, right_bottom]
    mine3 = [left_top, left_bottom]
    mine2 = [third(left_top, 1), third(right_bottom, -1)]

    picked = lax.dynamic_index_in_dim(negatives, column, 0, keepdims=False)
    route, route0 = routes(picked, per_block, ranks)
    number = lax.broadcasted_iota(jnp.int32, (queries, 1), 0) // per_block
    facts = jnp.concatenate(
        [jnp.ones_like(number), number, positives[:, None] // 16, positives[:, None] % 16], axis=1
    ).astype(BF16)
    lead = jnp.where(column == 0, 1.0, 0.0)
    facts = jnp.concatenate(
        [
            jnp.dot(route, facts, preferred_element_type=F32),
            jnp.sum(route0.astype(F32), axis=1, keepdims=True) * lead,
        ],
        axis=1,
    ).astype(BF16)
    facts = jnp.pad(facts, ((0, 0), (0, 128 - facts.shape[1])))
    outgoing = jnp.dot(route, query_states, preferred_element_type=F32).astype(BF16)
    outgoing = jnp.concatenate([outgoing, facts], axis=1)
    rows = outgoing.shape[0]
    asked = lax.all_to_all(
        outgoing.reshape(ranks, rows // ranks, depth + 128),
        "dp",
        split_axis=0,
        concat_axis=0,
        tiled=True,
    ).reshape(rows, depth + 128)
    facts = asked[:, depth : depth + 8].astype(jnp.int32).T
    valid = facts[0:1]
    block_of = facts[1]
    chosen = jnp.where(facts[4:5] == 1, facts[2:3] * 16 + facts[3:4], -1)

    other_states = swap(passage_last_states)
    other_asked = swap(asked)

    pieces = [
        (mine0, theirs0),
        (mine1, [swap(piece) for piece in mine1]),
        (mine2, [swap(piece) for piece in mine2]),
        (mine3, [swap(piece) for piece in mine3]),
    ]
    raws = [project(passage_last_states, asked, mine, theirs) for mine, theirs in pieces]
    emb, exps, scale, sums, hits = score(raws, chosen, valid)

    spread = (
        block_of.reshape(ranks, CAP, 1, per_block)
        == lax.broadcasted_iota(jnp.int32, (1, 1, blocks, 1), 2)
    ).astype(F32)
    both = jnp.concatenate([sums, hits], axis=0).reshape(2, ranks, CAP, 1, per_block)
    both = jnp.sum(both * spread[None], axis=2)
    packed = both.reshape(-1, blocks * per_block)
    packed = ring_sum(packed, first)
    packed = ring_sum(packed, second)
    packed = packed + swap(packed)
    packed = ring_sum(packed, third)
    both = packed.reshape(2, ranks, blocks, per_block)
    losses = (jnp.log(both[0]) - both[1]).reshape(-1)
    out_share = queries // groups
    loss_out = lax.dynamic_slice_in_dim(losses, (dp * groups + column) * out_share, out_share, 0)
    denom = jnp.sum(both[0][:, None] * spread, axis=2).reshape(1, rows)
    denom = jnp.where(valid == 1, denom, 1.0)
    d_mine, d_theirs = backward(emb, exps, scale, denom, chosen)

    d_other = swap(d_theirs)
    states = (passage_last_states, asked, other_states, other_asked)
    part = depth // SIDE
    terms = functools.partial(weight_terms, states, d_mine, d_other, u, part=part)
    far0, far1 = terms(items=[(2, 0), (2, 1)])
    from_left = first(far0, 1)
    from_right = first(far1, -1)
    right1, left0 = terms(items=[(1, 1), (3, 0)])
    left1_in = first(right1, 1)
    right0_in = first(left0, -1)
    right0, left1, own0, own1 = terms(items=[(1, 0), (3, 1), (0, 0), (0, 1)])
    left0_in = first(add(right0, from_left), 1)
    right1_in = first(add(left1, from_right), -1)
    summed = jnp.concatenate(
        [add(own0, left0_in, right0_in), add(own1, left1_in, right1_in)], axis=0
    )

    part2 = part // SIDE

    def chunk(step):
        return lax.dynamic_slice_in_dim(summed, lax.rem(v + step, SIDE) * part2, part2, 0)

    summed = add(
        chunk(0), second(chunk(1), 1), second(chunk(3), -1), second(chunk(2), 2)
    )
    cols = [summed[:, step * half : (step + 1) * half] for step in range(SIDE)]
    piece = add(cols[0], third(cols[1], 1), third(cols[3], -1), third(cols[2], 2))

    piece = jnp.concatenate(
        [piece, second(piece, -1), second(piece, 2), second(piece, 1)], axis=0
    )
    middle = piece.shape[0] // 2
    left = first(piece, 1)
    right = first(piece, -1)
    mine = [piece, right, first(left[:middle], 1), first(right[middle:], -1), left]
    other = [swap(block) for block in mine]
    return (loss_out, place_all(mine, other, u, v, core))


def solution(mesh):
    return jax.shard_map(
        shards,
        mesh=mesh,
        in_specs=(
            P("dp", None),
            P(("dp", "psg"), None),
            P(None, "psg"),
            P(None, "dp", None),
            P("dp"),
        ),
        out_specs=(P(("dp", "psg")), P(None, "psg")),
        check_vma=False,
    )
```

time: 373 us -> 487 us (1.31)
  Pallas kernels: 0 us -> 240 us
  matrix products: 111 us -> 2.19 us
  other arithmetic: 39.2 us -> 17.4 us
  local copies, waits for them, and re-layouts: 29.8 us -> 15.5 us
  waiting for transfers between devices: 111 us -> 120 us
  starting transfers between devices: 74.5 us -> 82.7 us
    pallas_call x0 -> x10, Pallas kernels: none -> 240 us  [the longest x1 129 us: place_all(): pl.pallas_call(place_kernel, in_specs=[pl.BlockSpec(memory_space=pltpu.SM...]
    dot_general x23 -> x0, matrix products: 107 us -> none  [the longest x16 66.6 us: project(): jnp.dot(states, piece, preferred_element_type=F32)]
    ppermute x11 -> x12, waiting for transfers between devices: 47 us -> 70.3 us  [third(): lax.ppermute(value, 'psg', [(c, (c + step) % SIDE) for c in range(SIDE)])]
    ppermute x11 -> x13, waiting for transfers between devices: 38.2 us -> 23.2 us  [first(): lax.ppermute(value, 'dp', dp_perm(lambda x, y, k: (x + step, y, k) if k =...]
    slice x14 -> x4, local copies, waits for them, and re-layouts: 12.4 us -> 0.18 us  [the longest x1 0.12 us: shards(): valid = facts[0:1]]
    ppermute x8 -> x15, starting transfers between devices: 22 us -> 33 us  [swap(): return lax.ppermute(value, 'dp', dp_perm(lambda x, y, k: (x, y, 1 - k)))]
    concatenate x8 -> x3, other arithmetic: 12.4 us -> 3.09 us  [the longest x1 3.05 us: shards(): jnp.concatenate([add(own0, left0_in, right0_in), add(own1, left1_in, righ...]
    convert_element_type x9 -> x6, other arithmetic: 13.6 us -> 7.75 us  [add(): return total.astype(BF16)]
  transfers between devices with their start and end apart: 42 -> 50, of which waited for: 24 -> 25; matrix products, arithmetic and copies ran while one was open for 35% -> 3% of each run, Pallas kernels for 0% -> 21%
where the time goes in v2:
time: 487 us; the launch traced here: 479 us
  Pallas kernels  240 us (49%)
  waiting for transfers between devices  120 us (25%)
  starting transfers between devices  82.7 us (17%)
  other arithmetic  17.4 us (4%)
  local copies, waits for them, and re-layouts  15.5 us (3%)
    pallas_call x1, Pallas kernels, place_all(): pl.pallas_call(place_kernel, in_specs=[pl.BlockSpec(memory_space=pltpu.SM...  129 us
    ppermute x12, waiting for transfers between devices, third(): lax.ppermute(value, 'psg', [(c, (c + step) % SIDE) for c in range(SIDE)])  70.3 us
    pallas_call x4, Pallas kernels, project(): pl.pallas_call(project_kernel, grid=(steps,), in_specs=[top, bottom, top,...  59.7 us
    ppermute x15, starting transfers between devices, swap(): return lax.ppermute(value, 'dp', dp_perm(lambda x, y, k: (x, y, 1 - k)))  33 us
    pallas_call x3, Pallas kernels, weight_terms(): pl.pallas_call(weight_kernel, grid_spec=grid_spec, out_shape=[jax.ShapeDt...  31.2 us
    ppermute x13, waiting for transfers between devices, first(): lax.ppermute(value, 'dp', dp_perm(lambda x, y, k: (x + step, y, k) if k =...  23.2 us
    ppermute x9, waiting for transfers between devices, second(): lax.ppermute(value, 'dp', dp_perm(lambda x, y, k: (x, y + step, k) if k =...  21.3 us
    ppermute x13, starting transfers between devices, first(): lax.ppermute(value, 'dp', dp_perm(lambda x, y, k: (x + step, y, k) if k =...  15.3 us
  transfers between devices with their start and end apart: 50, of which 25 were waited for; matrix products, arithmetic and copies ran while one was open for 3% of the time, Pallas kernels for 21%

profile of v2, /device:TPU:1, one launch (start us, length us, event | category | flops | bytes accessed | tf_op | source)
XLA Modules:
  0.0 478.8 jit_solution(5386500814553852095)
XLA Ops:
  6.1 2.3 fusion.1
  8.3 8.6 %all-to-all-start = ((bf16[32,16,4224]{2,1,0:T(8,128)(2,1)}), bf16[32,16,4224]{2,1,0:T(8,128)(2,1)}, u32[]{:S(2)}, u32[]{:S(2)}) async-start(bf16[32,16,4224]{2,1,0:T(8,128)(2,1)} %bitcast.44), calls=%async_computation | async-start | bytes 8650752 | tf_op jit(solution)/shard_map/all_to_all | solution.py:385
  17.0 3.4 constant_dynamic-slice_fusion.3
  22.0 2.1 collective-permute-start.1
  24.2 23.4 %collective-permute-done.4.mt = bf16[2048,256]{1,0:T(8,128)(2,1)S(1)} collective-permute-done((bf16[2048,256]{1,0:T(8,128)(2,1)S(1)}, bf16[2048,256]{1,0:T(8,128)(2,1)S(1)}, u32[]{:S(2)}, u32[]{:S(2)}) %collective-permute-start.4) | collective-permute-done | bytes 1048608 | tf_op jit(solution)/shard_map/ppermute | solution.py:42
  47.6 2.7 collective-permute-start.6
  50.3 2.5 collective-permute-start.10
  53.8 16.3 %collective-permute-done.9.mb = bf16[2048,256]{1,0:T(8,128)(2,1)} collective-permute-done((bf16[2048,256]{1,0:T(8,128)(2,1)S(1)}, bf16[2048,256]{1,0:T(8,128)(2,1)}, u32[]{:S(2)}, u32[]{:S(2)}) %collective-permute-start.9) | collective-permute-done | bytes 1048608 | tf_op jit(solution)/shard_map/ppermute | solution.py:42
  71.2 21.3 %collective-permute-done.5.mt = bf16[2048,256]{1,0:T(8,128)(2,1)} collective-permute-done((bf16[2048,256]{1,0:T(8,128)(2,1)S(1)}, bf16[2048,256]{1,0:T(8,128)(2,1)}, u32[]{:S(2)}, u32[]{:S(2)}) %collective-permute-start.5) | collective-permute-done | bytes 1048608 | tf_op jit(solution)/shard_map/ppermute | solution.py:42
  94.0 2.3 collective-permute-start.3
  98.5 14.8 %project.4.r0 = f32[1024,512]{1,0:T(8,128)} custom-call(bf16[512,4096]{1,0:T(8,128)(2,1)} %p.5, bf16[512,4096]{1,0:T(8,128)(2,1)} %p.5, bf16[512,4224]{1,0:T(8,128)(2,1)} %bitcast.6.qt.qb.q, bf16[512,4224]{1,0:T(8,128)(2,1)} %bitcast.6.qt.qb.q, bf16[2048,256]{1,0:T(8,128)(2,1)S(1)} %get-tuple-element.34.mt, bf16[2048,256]{1,0:T(8,128)(2,1)S(1)} %get-tuple-element.33.mb, ...), custom_call_target="tpu_custom_call" | custom-call | flops 4294967296 | bytes 14680064 | tf_op jit(solution)/shard_map/project/pallas_call | solution.py:89
  114.9 14.8 %project.7.r3 = f32[1024,512]{1,0:T(8,128)} custom-call(bf16[512,4096]{1,0:T(8,128)(2,1)} %p.5, bf16[512,4096]{1,0:T(8,128)(2,1)} %p.5, bf16[512,4224]{1,0:T(8,128)(2,1)} %bitcast.6.qt.qb.q, bf16[512,4224]{1,0:T(8,128)(2,1)} %bitcast.6.qt.qb.q, bf16[2048,256]{1,0:T(8,128)(2,1)S(1)} %copy-done.7, bf16[2048,256]{1,0:T(8,128)(2,1)} %collective-permute-done.9.mb, ...), custom_call_target="tpu_custom_call" | custom-call | flops 4294967296 | bytes 14680064 | tf_op jit(solution)/shard_map/project/pallas_call | solution.py:89
  130.0 15.0 %project.6.r2 = f32[1024,512]{1,0:T(8,128)} custom-call(bf16[512,4096]{1,0:T(8,128)(2,1)} %p.5, bf16[512,4096]{1,0:T(8,128)(2,1)} %p.5, bf16[512,4224]{1,0:T(8,128)(2,1)} %bitcast.6.qt.qb.q, bf16[512,4224]{1,0:T(8,128)(2,1)} %bitcast.6.qt.qb.q, bf16[2048,256]{1,0:T(8,128)(2,1)} %collective-permute-done.5.mt, bf16[2048,256]{1,0:T(8,128)(2,1)} %collective-permute-done.6.mb, ...), custom_call_target="tpu_custom_call" | custom-call | flops 4294967296 | bytes 14680064 | tf_op jit(solution)/shard_map/project/pallas_call | solution.py:89
  145.0 15.0 %project.5.r1 = f32[1024,512]{1,0:T(8,128)} custom-call(bf16[512,4096]{1,0:T(8,128)(2,1)} %p.5, bf16[512,4096]{1,0:T(8,128)(2,1)} %p.5, bf16[512,4224]{1,0:T(8,128)(2,1)} %bitcast.6.qt.qb.q, bf16[512,4224]{1,0:T(8,128)(2,1)} %bitcast.6.qt.qb.q, bf16[2048,256]{1,0:T(8,128)(2,1)} %collective-permute-done.mt, bf16[2048,256]{1,0:T(8,128)(2,1)} %collective-permute-done.1.mb, ...), custom_call_target="tpu_custom_call" | custom-call | flops 4294967296 | bytes 14680064 | tf_op jit(solution)/shard_map/project/pallas_call | solution.py:89
  163.2 10.2 %score.1 = (bf16[1024,2048]{1,0:T(8,128)(2,1)}, f32[512,512]{1,0:T(8,128)S(1)}, f32[1024,1]{1,0:T(8,128)S(1)}, f32[1,512]{1,0:T(1,128)S(1)}, f32[1,512]{1,0:T(1,128)S(1)}) custom-call(f32[1024,512]{1,0:T(8,128)S(1)} %copy-done.3, f32[1024,512]{1,0:T(8,128)S(1)} %copy-done.4, f32[1024,512]{1,0:T(8,128)} %project.6.r2, f32[1024,512]{1,0:T(8,128)} %project.7.r3, ...), custom_call_target="tpu_custom_call" | custom-call | flops 1073741824 | bytes 13631488 | tf_op jit(solution)/shard_map/score/pallas_call | solution.py:142
  179.3 2.7 collective-permute-done.14
  186.4 2.9 collective-permute-done.17
  189.3 3.7 collective-permute-start.18
  194.2 3.3 collective-permute-start.20
  198.7 3.0 collective-permute-done.21
  203.3 9.2 %backward.1 = (bf16[1024,1024]{1,0:T(8,128)(2,1)S(1)}, bf16[1024,1024]{1,0:T(8,128)(2,1)}) custom-call(bf16[1024,2048]{1,0:T(8,128)(2,1)} %get-tuple-element.19.emb, f32[512,512]{1,0:T(8,128)S(1)} %get-tuple-element.20.exps, f32[1024,1]{1,0:T(8,128)S(1)} %copy-done.11, f32[1,512]{1,0:T(1,128)S(1)} %copy.69.denom, s32[1,512]{1,0:T(1,128)S(1)} %copy.57.chosen), custom_call_target="tpu_custom_call" | custom-call | flops 2147483648 | bytes 9437184 | tf_op jit(solution)/shard_map/backward/pallas_call | solution.py:205
  212.5 2.0 collective-permute-start.24
  214.7 4.0 collective-permute-done.24.od
  218.6 8.0 %weight_terms.4 = (bf16[512,1024]{1,0:T(8,128)(2,1)S(1)}, bf16[512,1024]{1,0:T(8,128)(2,1)S(1)}) custom-call(s32[4]{0:T(128)S(1)} %get-tuple-element.51.cols, bf16[512,4096]{1,0:T(8,128)(2,1)} %p.5, bf16[512,4224]{1,0:T(8,128)(2,1)} %bitcast.6.qt.qb.q, bf16[512,4096]{1,0:T(8,128)(2,1)} %collective-permute-done.22.op, ...), custom_call_target="tpu_custom_call" | custom-call | flops 4294967296 | bytes 10485760 | tf_op jit(solution)/shard_map/weight_terms/pallas_call | solution.py:252
  228.0 8.9 %weight_terms.5 = (bf16[512,1024]{1,0:T(8,128)(2,1)}, bf16[512,1024]{1,0:T(8,128)(2,1)S(1)}) custom-call(s32[4]{0:T(128)S(1)} %get-tuple-element.52.cols, bf16[512,4096]{1,0:T(8,128)(2,1)} %p.5, bf16[512,4224]{1,0:T(8,128)(2,1)} %bitcast.6.qt.qb.q, bf16[512,4096]{1,0:T(8,128)(2,1)} %collective-permute-done.22.op, ...), custom_call_target="tpu_custom_call" | custom-call | flops 4294967296 | bytes 10485760 | tf_op jit(solution)/shard_map/weight_terms/pallas_call | solution.py:252
  237.2 14.3 %weight_terms.3 = (bf16[512,1024]{1,0:T(8,128)(2,1)S(1)}, bf16[512,1024]{1,0:T(8,128)(2,1)S(1)}, bf16[512,1024]{1,0:T(8,128)(2,1)S(1)}, bf16[512,1024]{1,0:T(8,128)(2,1)S(1)}) custom-call(s32[8]{0:T(128)S(1)} %stack.81.cols, bf16[512,4096]{1,0:T(8,128)(2,1)} %p.5, bf16[512,4224]{1,0:T(8,128)(2,1)} %bitcast.6.qt.qb.q, ...), custom_call_target="tpu_custom_call" | custom-call | flops 8589934592 | bytes 16777216 | tf_op jit(solution)/shard_map/weight_terms/pallas_call | solution.py:252
  252.9 2.6 collective-permute-start.30
  256.7 6.7 %collective-permute-done.25 = bf16[512,1024]{1,0:T(8,128)(2,1)S(1)} collective-permute-done((bf16[512,1024]{1,0:T(8,128)(2,1)S(1)}, bf16[512,1024]{1,0:T(8,128)(2,1)S(1)}, u32[]{:S(2)}, u32[]{:S(2)}) %collective-permute-start.25) | collective-permute-done | bytes 1048608 | tf_op jit(solution)/shard_map/ppermute | solution.py:30
  264.8 2.7 collective-permute-done.30
  267.5 2.2 add_convert_fusion
  269.7 9.0 %collective-permute-done.27 = bf16[512,1024]{1,0:T(8,128)(2,1)} collective-permute-done((bf16[512,1024]{1,0:T(8,128)(2,1)S(1)}, bf16[512,1024]{1,0:T(8,128)(2,1)}, u32[]{:S(2)}, u32[]{:S(2)}) %collective-permute-start.27) | collective-permute-done | bytes 1048608 | tf_op jit(solution)/shard_map/ppermute | solution.py:30
  280.3 2.2 add_convert_fusion.2
  282.5 3.0 fusion.4
  285.5 2.7 collective-permute-start.32
  288.2 7.1 %collective-permute-done.31 = bf16[256,1024]{1,0:T(8,128)(2,1)S(1)} collective-permute-done((bf16[256,1024]{1,0:T(8,128)(2,1)}, bf16[256,1024]{1,0:T(8,128)(2,1)S(1)}, u32[]{:S(2)}, u32[]{:S(2)}) %collective-permute-start.31) | collective-permute-done | bytes 524320 | tf_op jit(solution)/shard_map/ppermute | solution.py:36
  295.3 5.0 %collective-permute-done.32 = bf16[256,1024]{1,0:T(8,128)(2,1)S(1)} collective-permute-done((bf16[256,1024]{1,0:T(8,128)(2,1)}, bf16[256,1024]{1,0:T(8,128)(2,1)S(1)}, u32[]{:S(2)}, u32[]{:S(2)}) %collective-permute-start.32) | collective-permute-done | bytes 524320 | tf_op jit(solution)/shard_map/ppermute | solution.py:36
  301.8 2.7 collective-permute-start.35
  304.6 2.2 collective-permute-done.34
  307.8 2.3 collective-permute-done.36
  310.2 3.7 collective-permute-start.37
  314.6 2.6 collective-permute-done.37
  317.2 2.1 collective-permute-done.38
  321.3 1.8 collective-permute-start.40
  323.1 8.2 %collective-permute-start.44 = (bf16[1024,256]{1,0:T(8,128)(2,1)S(1)}, bf16[1024,256]{1,0:T(8,128)(2,1)S(1)}, u32[]{:S(2)}, u32[]{:S(2)}) collective-permute-start(bf16[1024,256]{1,0:T(8,128)(2,1)S(1)} %pad_maximum_fusion.refs_0_), channel_id=1, source_target_pairs={{0,4},{4,0},{8,12},{12,8},{16,20},{20,16},{24,28},{28,24},{32,36},... | collective-permute-start | bytes 1572872 | tf_op jit(solution)/shard_map/ppermute | solution.py:46
  332.0 2.7 collective-permute-start.43
  334.7 7.2 %collective-permute-start.45 = (bf16[1024,256]{1,0:T(8,128)(2,1)S(1)}, bf16[1024,256]{1,0:T(8,128)(2,1)S(1)}, u32[]{:S(2)}, u32[]{:S(2)}) collective-permute-start(bf16[1024,256]{1,0:T(8,128)(2,1)S(1)} %collective-permute-done.40.refs_1_), channel_id=1, source_target_pairs={{0,4},{4,0},{8,12},{12,8},{16,20},{20,16},{24,28},{28,24},{32,36},... | collective-permute-start | bytes 1572872 | tf_op jit(solution)/shard_map/ppermute | solution.py:46
  341.9 4.2 collective-permute-start.46
  349.1 129.3 %place_all.1 = bf16[4096,512]{1,0:T(8,128)(2,1)} custom-call(s32[3]{0:T(128)} %pad_add_fusion.places, bf16[1024,256]{1,0:T(8,128)(2,1)} %copy-done.13, bf16[1024,256]{1,0:T(8,128)(2,1)} %copy-done.15, bf16[512,256]{1,0:T(8,128)(2,1)} %copy-done.18, bf16[512,256]{1,0:T(8,128)(2,1)} %copy-done.19, bf16[1024,256]{1,0:T(8,128)(2,1)} %copy-done.14, ...), custom_call_target="tpu_custom_call" | custom-call | tf_op jit(solution)/shard_map/place_all/pallas_call | solution.py:300
  (167 shorter events, 48.4 us)
Async XLA Ops:
  8.3 89.0 %all-to-all-start = ((bf16[32,16,4224]{2,1,0:T(8,128)(2,1)}), bf16[32,16,4224]{2,1,0:T(8,128)(2,1)}, u32[]{:S(2)}, u32[]{:S(2)}) async-start(bf16[32,16,4224]{2,1,0:T(8,128)(2,1)} %bitcast.44), calls=%async_computation | async-start | bytes 8650752 | tf_op jit(solution)/shard_map/all_to_all | solution.py:385
  20.4 27.2 %collective-permute-start.4 = (bf16[2048,256]{1,0:T(8,128)(2,1)S(1)}, bf16[2048,256]{1,0:T(8,128)(2,1)S(1)}, u32[]{:S(2)}, u32[]{:S(2)}) collective-permute-start(bf16[2048,256]{1,0:T(8,128)(2,1)S(1)} %get-tuple-element.34.mt), channel_id=1, source_target_pairs={{0,1},{1,2},{2,3},{3,0},{4,5},{5,6},{6,7},{7,4},{8,9},{9,10},{10,1... | collective-permute-start | bytes 3145736 | tf_op jit(solution)/shard_map/ppermute | solution.py:42
  22.0 25.5 %collective-permute-start.1 = (bf16[2048,256]{1,0:T(8,128)(2,1)S(1)}, bf16[2048,256]{1,0:T(8,128)(2,1)}, u32[]{:S(2)}, u32[]{:S(2)}) collective-permute-start(bf16[2048,256]{1,0:T(8,128)(2,1)S(1)} %get-tuple-element.33.mb), channel_id=1, source_target_pairs={{0,3},{1,0},{2,1},{3,2},{4,7},{5,4},{6,5},{7,6},{8,11},{9,8},{10,9... | collective-permute-start | bytes 3145736 | tf_op jit(solution)/shard_map/ppermute | solution.py:42
  24.2 45.9 %collective-permute-start.9 = (bf16[2048,256]{1,0:T(8,128)(2,1)S(1)}, bf16[2048,256]{1,0:T(8,128)(2,1)}, u32[]{:S(2)}, u32[]{:S(2)}) collective-permute-start(bf16[2048,256]{1,0:T(8,128)(2,1)S(1)} %get-tuple-element.33.mb), channel_id=1, source_target_pairs={{0,1},{1,2},{2,3},{3,0},{4,5},{5,6},{6,7},{7,4},{8,9},{9,10},{10,1... | collective-permute-start | bytes 3145736 | tf_op jit(solution)/shard_map/ppermute | solution.py:42
  47.6 44.9 %collective-permute-start.5 = (bf16[2048,256]{1,0:T(8,128)(2,1)S(1)}, bf16[2048,256]{1,0:T(8,128)(2,1)}, u32[]{:S(2)}, u32[]{:S(2)}) collective-permute-start(bf16[2048,256]{1,0:T(8,128)(2,1)S(1)} %collective-permute-done.4.mt), channel_id=1, source_target_pairs={{0,1},{1,2},{2,3},{3,0},{4,5},{5,6},{6,7},{7,4},{8,9},{9,10},{10,1... | collective-permute-start | bytes 3145736 | tf_op jit(solution)/shard_map/ppermute | solution.py:42
  47.6 45.7 %collective-permute-start.6 = (bf16[2048,256]{1,0:T(8,128)(2,1)}, bf16[2048,256]{1,0:T(8,128)(2,1)}, u32[]{:S(2)}, u32[]{:S(2)}) collective-permute-start(bf16[2048,256]{1,0:T(8,128)(2,1)} %collective-permute-done.1.mb), channel_id=1, source_target_pairs={{0,3},{1,0},{2,1},{3,2},{4,7},{5,4},{6,5},{7,6},{8,11},{9,8},{10,9... | collective-permute-start | bytes 3145736 | tf_op jit(solution)/shard_map/ppermute | solution.py:42
  50.3 43.8 %collective-permute-start = (bf16[2048,256]{1,0:T(8,128)(2,1)S(1)}, bf16[2048,256]{1,0:T(8,128)(2,1)}, u32[]{:S(2)}, u32[]{:S(2)}) collective-permute-start(bf16[2048,256]{1,0:T(8,128)(2,1)S(1)} %get-tuple-element.34.mt), channel_id=1, source_target_pairs={{0,3},{1,0},{2,1},{3,2},{4,7},{5,4},{6,5},{7,6},{8,11},{9,8},{10,9... | collective-permute-start | bytes 3145736 | tf_op jit(solution)/shard_map/ppermute | solution.py:42
  50.3 46.0 %collective-permute-start.10 = (bf16[2048,256]{1,0:T(8,128)(2,1)S(1)}, bf16[2048,256]{1,0:T(8,128)(2,1)S(1)}, u32[]{:S(2)}, u32[]{:S(2)}) collective-permute-start(bf16[2048,256]{1,0:T(8,128)(2,1)S(1)} %collective-permute-done.4.mt), channel_id=1, source_target_pairs={{0,4},{4,0},{8,12},{12,8},{16,20},{20,16},{24,28},{28,24},{32,36},... | collective-permute-start | bytes 3145736 | tf_op jit(solution)/shard_map/ppermute | solution.py:46
  70.0 44.3 %collective-permute-start.11 = (bf16[2048,256]{1,0:T(8,128)(2,1)}, bf16[2048,256]{1,0:T(8,128)(2,1)}, u32[]{:S(2)}, u32[]{:S(2)}) collective-permute-start(bf16[2048,256]{1,0:T(8,128)(2,1)} %collective-permute-done.9.mb), channel_id=1, source_target_pairs={{0,4},{4,0},{8,12},{12,8},{16,20},{20,16},{24,28},{28,24},{32,36},... | collective-permute-start | bytes 3145736 | tf_op jit(solution)/shard_map/ppermute | solution.py:46
  92.5 37.2 %collective-permute-start.7 = (bf16[2048,256]{1,0:T(8,128)(2,1)}, bf16[2048,256]{1,0:T(8,128)(2,1)}, u32[]{:S(2)}, u32[]{:S(2)}) collective-permute-start(bf16[2048,256]{1,0:T(8,128)(2,1)} %collective-permute-done.5.mt), channel_id=1, source_target_pairs={{0,4},{4,0},{8,12},{12,8},{16,20},{20,16},{24,28},{28,24},{32,36},... | collective-permute-start | bytes 3145736 | tf_op jit(solution)/shard_map/ppermute | solution.py:46
  93.3 36.6 %collective-permute-start.8 = (bf16[2048,256]{1,0:T(8,128)(2,1)}, bf16[2048,256]{1,0:T(8,128)(2,1)}, u32[]{:S(2)}, u32[]{:S(2)}) collective-permute-start(bf16[2048,256]{1,0:T(8,128)(2,1)} %collective-permute-done.6.mb), channel_id=1, source_target_pairs={{0,4},{4,0},{8,12},{12,8},{16,20},{20,16},{24,28},{28,24},{32,36},... | collective-permute-start | bytes 3145736 | tf_op jit(solution)/shard_map/ppermute | solution.py:46
  94.0 51.0 %collective-permute-start.3 = (bf16[2048,256]{1,0:T(8,128)(2,1)}, bf16[2048,256]{1,0:T(8,128)(2,1)}, u32[]{:S(2)}, u32[]{:S(2)}) collective-permute-start(bf16[2048,256]{1,0:T(8,128)(2,1)} %collective-permute-done.1.mb), channel_id=1, source_target_pairs={{0,4},{4,0},{8,12},{12,8},{16,20},{20,16},{24,28},{28,24},{32,36},... | collective-permute-start | bytes 3145736 | tf_op jit(solution)/shard_map/ppermute | solution.py:46
  97.3 47.7 %collective-permute-start.2 = (bf16[2048,256]{1,0:T(8,128)(2,1)}, bf16[2048,256]{1,0:T(8,128)(2,1)}, u32[]{:S(2)}, u32[]{:S(2)}) collective-permute-start(bf16[2048,256]{1,0:T(8,128)(2,1)} %collective-permute-done.mt), channel_id=1, source_target_pairs={{0,4},{4,0},{8,12},{12,8},{16,20},{20,16},{24,28},{28,24},{32,36},... | collective-permute-start | bytes 3145736 | tf_op jit(solution)/shard_map/ppermute | solution.py:46
  114.3 100.4 %collective-permute-start.22 = (bf16[512,4096]{1,0:T(8,128)(2,1)}, bf16[512,4096]{1,0:T(8,128)(2,1)}, u32[]{:S(2)}, u32[]{:S(2)}) collective-permute-start(bf16[512,4096]{1,0:T(8,128)(2,1)} %p.5), channel_id=1, source_target_pairs={{0,4},{4,0},{8,12},{12,8},{16,20},{20,16},{24,28},{28,24},{32,36},... | collective-permute-start | bytes 12582920 | tf_op jit(solution)/shard_map/ppermute | solution.py:46
  129.8 88.9 %collective-permute-start.23 = (bf16[512,4224]{1,0:T(8,128)(2,1)}, bf16[512,4224]{1,0:T(8,128)(2,1)}, u32[]{:S(2)}, u32[]{:S(2)}) collective-permute-start(bf16[512,4224]{1,0:T(8,128)(2,1)} %bitcast.6.qt.qb.q), channel_id=1, source_target_pairs={{0,4},{4,0},{8,12},{12,8},{16,20},{20,16},{24,28},{28,24},{32,36},... | collective-permute-start | bytes 12976136 | tf_op jit(solution)/shard_map/ppermute | solution.py:46
  175.0 4.3 collective-permute-start.12
  176.4 3.0 collective-permute-start.13
  177.7 4.3 collective-permute-start.14
  182.0 4.4 collective-permute-start.15
  185.0 4.3 collective-permute-start.17
  189.3 4.6 collective-permute-start.18
  193.9 4.8 %collective-permute-start.19 = (f32[64,128]{1,0:T(8,128)S(1)}, f32[64,128]{1,0:T(8,128)S(1)}, u32[]{:S(2)}, u32[]{:S(2)}) collective-permute-start(f32[64,128]{1,0:T(8,128)S(1)} %add.213), channel_id=1, source_target_pairs={{0,1},{1,2},{2,3},{3,0},{4,5},{5,6},{6,7},{7,4},{8,9},{9,10},{10,1... | collective-permute-start | bytes 98312 | tf_op jit(solution)/shard_map/ppermute | solution.py:42
  194.2 4.5 collective-permute-start.20
  197.5 4.3 collective-permute-start.21
  212.5 6.1 %collective-permute-start.24 = (bf16[1024,1024]{1,0:T(8,128)(2,1)}, bf16[1024,1024]{1,0:T(8,128)(2,1)}, u32[]{:S(2)}, u32[]{:S(2)}) collective-permute-start(bf16[1024,1024]{1,0:T(8,128)(2,1)} %get-tuple-element.23), channel_id=1, source_target_pairs={{0,4},{4,0},{8,12},{12,8},{16,20},{20,16},{24,28},{28,24},{32,36},... | collective-permute-start | bytes 6291464 | tf_op jit(solution)/shard_map/ppermute | solution.py:46
  226.7 24.8 %collective-permute-start.29 = (bf16[512,1024]{1,0:T(8,128)(2,1)S(1)}, bf16[512,1024]{1,0:T(8,128)(2,1)S(1)}, u32[]{:S(2)}, u32[]{:S(2)}) collective-permute-start(bf16[512,1024]{1,0:T(8,128)(2,1)S(1)} %get-tuple-element.31), channel_id=1, source_target_pairs={{0,96},{4,28},{8,104},{12,4},{16,112},{20,12},{24,120},{28,20},{32... | collective-permute-start | bytes 3145736 | tf_op jit(solution)/shard_map/ppermute | solution.py:30
  236.8 28.0 %collective-permute-start.28 = (bf16[512,1024]{1,0:T(8,128)(2,1)}, bf16[512,1024]{1,0:T(8,128)(2,1)}, u32[]{:S(2)}, u32[]{:S(2)}) collective-permute-start(bf16[512,1024]{1,0:T(8,128)(2,1)} %get-tuple-element.29), channel_id=1, source_target_pairs={{0,32},{4,12},{8,40},{12,20},{16,48},{20,28},{24,56},{28,4},{32,64... | collective-permute-start | bytes 3145736 | tf_op jit(solution)/shard_map/ppermute | solution.py:30
  237.1 26.3 %collective-permute-start.25 = (bf16[512,1024]{1,0:T(8,128)(2,1)S(1)}, bf16[512,1024]{1,0:T(8,128)(2,1)S(1)}, u32[]{:S(2)}, u32[]{:S(2)}) collective-permute-start(bf16[512,1024]{1,0:T(8,128)(2,1)S(1)} %get-tuple-element.26), channel_id=1, source_target_pairs={{0,32},{4,12},{8,40},{12,20},{16,48},{20,28},{24,56},{28,4},{32,64... | collective-permute-start | bytes 3145736 | tf_op jit(solution)/shard_map/ppermute | solution.py:30
  252.9 14.6 %collective-permute-start.30 = (bf16[512,1024]{1,0:T(8,128)(2,1)}, bf16[512,1024]{1,0:T(8,128)(2,1)}, u32[]{:S(2)}, u32[]{:S(2)}) collective-permute-start(bf16[512,1024]{1,0:T(8,128)(2,1)} %add_convert_fusion.1), channel_id=1, source_target_pairs={{0,96},{4,28},{8,104},{12,4},{16,112},{20,12},{24,120},{28,20},{32... | collective-permute-start | bytes 3145736 | tf_op jit(solution)/shard_map/ppermute | solution.py:30
  255.5 23.2 %collective-permute-start.27 = (bf16[512,1024]{1,0:T(8,128)(2,1)S(1)}, bf16[512,1024]{1,0:T(8,128)(2,1)}, u32[]{:S(2)}, u32[]{:S(2)}) collective-permute-start(bf16[512,1024]{1,0:T(8,128)(2,1)S(1)} %get-tuple-element.27), channel_id=1, source_target_pairs={{0,96},{4,28},{8,104},{12,4},{16,112},{20,12},{24,120},{28,20},{32... | collective-permute-start | bytes 3145736 | tf_op jit(solution)/shard_map/ppermute | solution.py:30
  264.8 15.5 %collective-permute-start.26 = (bf16[512,1024]{1,0:T(8,128)(2,1)}, bf16[512,1024]{1,0:T(8,128)(2,1)}, u32[]{:S(2)}, u32[]{:S(2)}) collective-permute-start(bf16[512,1024]{1,0:T(8,128)(2,1)} %add_convert_fusion.3), channel_id=1, source_target_pairs={{0,32},{4,12},{8,40},{12,20},{16,48},{20,28},{24,56},{28,4},{32,64... | collective-permute-start | bytes 3145736 | tf_op jit(solution)/shard_map/ppermute | solution.py:30
  285.5 9.8 %collective-permute-start.31 = (bf16[256,1024]{1,0:T(8,128)(2,1)}, bf16[256,1024]{1,0:T(8,128)(2,1)S(1)}, u32[]{:S(2)}, u32[]{:S(2)}) collective-permute-start(bf16[256,1024]{1,0:T(8,128)(2,1)} %get-tuple-element.36), channel_id=1, source_target_pairs={{0,8},{4,36},{8,16},{12,44},{16,24},{20,52},{24,0},{28,60},{32,40}... | collective-permute-start | bytes 1572872 | tf_op jit(solution)/shard_map/ppermute | solution.py:36
  285.5 14.7 %collective-permute-start.32 = (bf16[256,1024]{1,0:T(8,128)(2,1)}, bf16[256,1024]{1,0:T(8,128)(2,1)S(1)}, u32[]{:S(2)}, u32[]{:S(2)}) collective-permute-start(bf16[256,1024]{1,0:T(8,128)(2,1)} %get-tuple-element.37), channel_id=1, source_target_pairs={{0,24},{4,100},{8,0},{12,108},{16,8},{20,116},{24,16},{28,124},{32... | collective-permute-start | bytes 1572872 | tf_op jit(solution)/shard_map/ppermute | solution.py:36
  288.2 12.6 %collective-permute-start.33 = (bf16[256,1024]{1,0:T(8,128)(2,1)S(1)}, bf16[256,1024]{1,0:T(8,128)(2,1)S(1)}, u32[]{:S(2)}, u32[]{:S(2)}) collective-permute-start(bf16[256,1024]{1,0:T(8,128)(2,1)S(1)} %get-tuple-element.38), channel_id=1, source_target_pairs={{0,16},{4,68},{8,24},{12,76},{16,0},{20,84},{24,8},{28,92},{32,48}... | collective-permute-start | bytes 1572872 | tf_op jit(solution)/shard_map/ppermute | solution.py:36
  301.5 5.4 %collective-permute-start.34 = (bf16[256,256]{1,0:T(8,128)(2,1)S(1)}, bf16[256,256]{1,0:T(8,128)(2,1)S(1)}, u32[]{:S(2)}, u32[]{:S(2)}) collective-permute-start(bf16[256,256]{1,0:T(8,128)(2,1)S(1)} %get-tuple-element.39), channel_id=1, source_target_pairs={{0,1},{1,2},{2,3},{3,0},{4,5},{5,6},{6,7},{7,4},{8,9},{9,10},{10,1... | collective-permute-start | bytes 393224 | tf_op jit(solution)/shard_map/ppermute | solution.py:42
  301.8 6.0 %collective-permute-start.35 = (bf16[256,256]{1,0:T(8,128)(2,1)S(1)}, bf16[256,256]{1,0:T(8,128)(2,1)S(1)}, u32[]{:S(2)}, u32[]{:S(2)}) collective-permute-start(bf16[256,256]{1,0:T(8,128)(2,1)S(1)} %get-tuple-element.41), channel_id=1, source_target_pairs={{0,3},{1,0},{2,1},{3,2},{4,7},{5,4},{6,5},{7,6},{8,11},{9,8},{10,9... | collective-permute-start | bytes 393224 | tf_op jit(solution)/shard_map/ppermute | solution.py:42
  304.4 5.6 %collective-permute-start.36 = (bf16[256,256]{1,0:T(8,128)(2,1)S(1)}, bf16[256,256]{1,0:T(8,128)(2,1)S(1)}, u32[]{:S(2)}, u32[]{:S(2)}) collective-permute-start(bf16[256,256]{1,0:T(8,128)(2,1)S(1)} %get-tuple-element.40), channel_id=1, source_target_pairs={{0,2},{1,3},{2,0},{3,1},{4,6},{5,7},{6,4},{7,5},{8,10},{9,11},{10,... | collective-permute-start | bytes 393224 | tf_op jit(solution)/shard_map/ppermute | solution.py:42
  310.2 7.0 %collective-permute-start.37 = (bf16[256,256]{1,0:T(8,128)(2,1)S(1)}, bf16[256,256]{1,0:T(8,128)(2,1)S(1)}, u32[]{:S(2)}, u32[]{:S(2)}) collective-permute-start(bf16[256,256]{1,0:T(8,128)(2,1)S(1)} %add_convert_fusion.5), channel_id=1, source_target_pairs={{0,24},{4,100},{8,0},{12,108},{16,8},{20,116},{24,16},{28,124},{32... | collective-permute-start | bytes 393224 | tf_op jit(solution)/shard_map/ppermute | solution.py:36
  313.9 5.4 %collective-permute-start.38 = (bf16[256,256]{1,0:T(8,128)(2,1)S(1)}, bf16[256,256]{1,0:T(8,128)(2,1)S(1)}, u32[]{:S(2)}, u32[]{:S(2)}) collective-permute-start(bf16[256,256]{1,0:T(8,128)(2,1)S(1)} %add_convert_fusion.5), channel_id=1, source_target_pairs={{0,16},{4,68},{8,24},{12,76},{16,0},{20,84},{24,8},{28,92},{32,48}... | collective-permute-start | bytes 393224 | tf_op jit(solution)/shard_map/ppermute | solution.py:36
  313.9 6.4 %collective-permute-start.39 = (bf16[256,256]{1,0:T(8,128)(2,1)S(1)}, bf16[256,256]{1,0:T(8,128)(2,1)S(1)}, u32[]{:S(2)}, u32[]{:S(2)}) collective-permute-start(bf16[256,256]{1,0:T(8,128)(2,1)S(1)} %add_convert_fusion.5), channel_id=1, source_target_pairs={{0,8},{4,36},{8,16},{12,44},{16,24},{20,52},{24,0},{28,60},{32,40}... | collective-permute-start | bytes 393224 | tf_op jit(solution)/shard_map/ppermute | solution.py:36
  320.4 11.5 %collective-permute-start.41 = (bf16[1024,256]{1,0:T(8,128)(2,1)S(1)}, bf16[1024,256]{1,0:T(8,128)(2,1)S(1)}, u32[]{:S(2)}, u32[]{:S(2)}) collective-permute-start(bf16[1024,256]{1,0:T(8,128)(2,1)S(1)} %pad_maximum_fusion.refs_0_), channel_id=1, source_target_pairs={{0,32},{4,12},{8,40},{12,20},{16,48},{20,28},{24,56},{28,4},{32,64... | collective-permute-start | bytes 1572872 | tf_op jit(solution)/shard_map/ppermute | solution.py:30
  321.3 10.7 %collective-permute-start.40 = (bf16[1024,256]{1,0:T(8,128)(2,1)S(1)}, bf16[1024,256]{1,0:T(8,128)(2,1)S(1)}, u32[]{:S(2)}, u32[]{:S(2)}) collective-permute-start(bf16[1024,256]{1,0:T(8,128)(2,1)S(1)} %pad_maximum_fusion.refs_0_), channel_id=1, source_target_pairs={{0,96},{4,28},{8,104},{12,4},{16,112},{20,12},{24,120},{28,20},{32... | collective-permute-start | bytes 1572872 | tf_op jit(solution)/shard_map/ppermute | solution.py:30
  323.1 24.4 %collective-permute-start.44 = (bf16[1024,256]{1,0:T(8,128)(2,1)S(1)}, bf16[1024,256]{1,0:T(8,128)(2,1)S(1)}, u32[]{:S(2)}, u32[]{:S(2)}) collective-permute-start(bf16[1024,256]{1,0:T(8,128)(2,1)S(1)} %pad_maximum_fusion.refs_0_), channel_id=1, source_target_pairs={{0,4},{4,0},{8,12},{12,8},{16,20},{20,16},{24,28},{28,24},{32,36},... | collective-permute-start | bytes 1572872 | tf_op jit(solution)/shard_map/ppermute | solution.py:46
  331.9 10.1 %collective-permute-start.42 = (bf16[512,256]{1,0:T(8,128)(2,1)S(1)}, bf16[512,256]{1,0:T(8,128)(2,1)S(1)}, u32[]{:S(2)}, u32[]{:S(2)}) collective-permute-start(bf16[512,256]{1,0:T(8,128)(2,1)S(1)} %slice.79), channel_id=1, source_target_pairs={{0,32},{4,12},{8,40},{12,20},{16,48},{20,28},{24,56},{28,4},{32,64... | collective-permute-start | bytes 786440 | tf_op jit(solution)/shard_map/ppermute | solution.py:30
  332.0 14.2 %collective-permute-start.43 = (bf16[512,256]{1,0:T(8,128)(2,1)S(1)}, bf16[512,256]{1,0:T(8,128)(2,1)S(1)}, u32[]{:S(2)}, u32[]{:S(2)}) collective-permute-start(bf16[512,256]{1,0:T(8,128)(2,1)S(1)} %slice.80), channel_id=1, source_target_pairs={{0,96},{4,28},{8,104},{12,4},{16,112},{20,12},{24,120},{28,20},{32... | collective-permute-start | bytes 786440 | tf_op jit(solution)/shard_map/ppermute | solution.py:30
  334.7 13.1 %collective-permute-start.45 = (bf16[1024,256]{1,0:T(8,128)(2,1)S(1)}, bf16[1024,256]{1,0:T(8,128)(2,1)S(1)}, u32[]{:S(2)}, u32[]{:S(2)}) collective-permute-start(bf16[1024,256]{1,0:T(8,128)(2,1)S(1)} %collective-permute-done.40.refs_1_), channel_id=1, source_target_pairs={{0,4},{4,0},{8,12},{12,8},{16,20},{20,16},{24,28},{28,24},{32,36},... | collective-permute-start | bytes 1572872 | tf_op jit(solution)/shard_map/ppermute | solution.py:46
  341.9 7.1 %collective-permute-start.48 = (bf16[1024,256]{1,0:T(8,128)(2,1)S(1)}, bf16[1024,256]{1,0:T(8,128)(2,1)}, u32[]{:S(2)}, u32[]{:S(2)}) collective-permute-start(bf16[1024,256]{1,0:T(8,128)(2,1)S(1)} %collective-permute-done.41.refs_4_), channel_id=1, source_target_pairs={{0,4},{4,0},{8,12},{12,8},{16,20},{20,16},{24,28},{28,24},{32,36},... | collective-permute-start | bytes 1572872 | tf_op jit(solution)/shard_map/ppermute | solution.py:46
  341.9 5.6 %collective-permute-start.46 = (bf16[512,256]{1,0:T(8,128)(2,1)S(1)}, bf16[512,256]{1,0:T(8,128)(2,1)S(1)}, u32[]{:S(2)}, u32[]{:S(2)}) collective-permute-start(bf16[512,256]{1,0:T(8,128)(2,1)S(1)} %collective-permute-done.42.refs_2_), channel_id=1, source_target_pairs={{0,4},{4,0},{8,12},{12,8},{16,20},{20,16},{24,28},{28,24},{32,36},... | collective-permute-start | bytes 786440 | tf_op jit(solution)/shard_map/ppermute | solution.py:46
  (23 other events, 281.7 us)
